TPU v7x, 32 devices: a whole 2x2x4 slice. The times are simulated.
32 devices in a mesh: ha: 8 (over y, x, core), wa: 4 (over z).
Axes of the slice: x: 2, y: 2, z: 4, core: 2. Of those that a mesh axis runs over, the one named last changes fastest.
Arguments:
- frames: bfloat16 [2, 128, 256, 384], P(None, 'ha', 'wa'), may hold values from -6 to 6
- keep: int32 [2, 3], replicated, may hold values 0 or 1
- expand_weight: bfloat16 [384, 1536], replicated, may hold values from -0.3125 to 0.3125
- dw_kernel: float32 [3, 3, 1536], replicated, may hold values from -2 to 2
- conv_bias: float32 [1536], replicated, may hold values from -3 to 3
- project_weight: bfloat16 [1536, 384], replicated, may hold values from -0.15625 to 0.15625
- qkv_weight: bfloat16 [384, 1152], replicated, may hold values from -4 to 4
- out_weight: bfloat16 [384, 384], replicated, may hold values from -0.3125 to 0.3125
- mlp_in: bfloat16 [384, 1536], replicated, may hold values from -0.3125 to 0.3125
- mlp_out: bfloat16 [1536, 384], replicated, may hold values from -0.15625 to 0.15625
Outputs:
- result: bfloat16 [2, 128, 256, 384], P(None, 'ha', 'wa')
All inputs are finite; a program needn't handle non-finite values.
Results may differ from a plain program's by a relative error of at most 0.0068.
Values may be sent and summed in bfloat16 or wider, within the bound.
No kernel may reach another device: no remote copies, remote signals or barrier semaphores. Data moves between devices by JAX's collectives and lax.ppermute only.
A program may use at most 64 MiB of HBM per device.

v0:
```python
import math

import jax
import jax.numpy as jnp
import numpy as np
from jax import lax
from jax.experimental import pallas as pl
from jax.experimental.pallas import tpu as pltpu
from jax.sharding import PartitionSpec as P

HEADS = 12
GRID = 16
SEG = 8
CHUNK = 768
F32 = jnp.float32
BF16 = jnp.bfloat16
MIB = 1024 * 1024


def gelu(v):
    cubic = v * (math.sqrt(2 / math.pi) + (math.sqrt(2 / math.pi) * 0.044715) * (v * v))
    half = 0.5 * v
    return half + half * jnp.tanh(cubic)


def half_gelu(h):
    root = math.sqrt(2 / math.pi)
    return h + h * jnp.tanh(h * (2 * root + (8 * root * 0.044715) * (h * h)))


def normalize(values):
    mean_val = jnp.mean(values, axis=-1, keepdims=True)
    centred = values - mean_val
    variance = jnp.mean(centred * centred, axis=-1, keepdims=True)
    return centred * lax.rsqrt(variance + 1e-05)


def dot(a, b):
    return jnp.dot(a, b, preferred_element_type=F32)


def dot_t(a, b):
    return lax.dot_general(a, b, (((1,), (1,)), ((), ())), preferred_element_type=F32)


def segment_order(cols, count):
    steps = cols // SEG
    matrix = np.zeros((count * cols, count * cols), np.float32)
    for row in range(count):
        for t in range(steps):
            for s in range(SEG):
                matrix[row * cols + t * SEG + s, row * cols + s * steps + t] = 1
    return matrix


def message_order(row_groups, cols, col_stride, cols_each):
    col_groups = cols // col_stride
    dests = col_stride // cols_each
    matrix = np.zeros((row_groups * cols, row_groups * cols), np.float32)
    place = 0
    for w in range(dests):
        for b in range(cols_each):
            for g in range(row_groups):
                for h in range(col_groups):
                    matrix[place, g * cols + h * col_stride + w * cols_each + b] = 1
                    place += 1
    return matrix


def expand_kernel(frame, seg_any, x_any, expand_any, expanded, tokens, x_ref, expand_ref, seg_ref, sems):
    rows, steps, _, hidden = expanded.shape
    cols = steps * SEG
    channels = x_ref.shape[-1]
    pairs = [(seg_any, seg_ref), (x_any.at[frame], x_ref), (expand_any, expand_ref)]
    copies = [pltpu.make_async_copy(src, dst, sems.at[i]) for i, (src, dst) in enumerate(pairs)]
    for copy in copies:
        copy.start()
    copies[0].wait()
    copies[1].wait()
    pair = 2 * cols
    for r in range(rows // 2):
        both = x_ref[2 * r : 2 * r + 2].reshape(pair, channels)
        tokens[r * pair : (r + 1) * pair] = dot(seg_ref[...], both).astype(BF16)
    copies[2].wait()
    block = 4
    for c in range(hidden // CHUNK):
        lanes = slice(c * CHUNK, (c + 1) * CHUNK)
        for r in range(0, rows, block):
            value = half_gelu(dot(tokens[r * cols : (r + block) * cols], expand_ref[:, lanes]))
            expanded[r : r + block, :, :, lanes] = value.reshape(block, steps, SEG, CHUNK)


def expand_call(frame, seg, x, expand_weight):
    _, rows, cols, channels = x.shape
    hidden = expand_weight.shape[1]

    def body(*refs):
        expand_kernel(frame, *refs)

    return pl.pallas_call(
        body,
        in_specs=[pl.BlockSpec(memory_space=pl.ANY)] * 3,
        out_specs=[pl.BlockSpec(memory_space=pltpu.VMEM)] * 2,
        out_shape=[
            jax.ShapeDtypeStruct((rows, cols // SEG, SEG, hidden), F32),
            jax.ShapeDtypeStruct((rows * cols, channels), BF16),
        ],
        scratch_shapes=[
            pltpu.VMEM(x.shape[1:], BF16),
            pltpu.VMEM(expand_weight.shape, BF16),
            pltpu.VMEM(seg.shape, BF16),
            pltpu.SemaphoreType.DMA((3,)),
        ],
        compiler_params=pltpu.CompilerParams(vmem_limit_bytes=24 * MIB),
        cost_estimate=pl.CostEstimate(flops=3 * 10**9, bytes_accessed=4 * 10**6, transcendentals=2 * 10**6),
    )(seg, x, expand_weight)


def conv_kernel(
    frame,
    keep_ref,
    even_ref,
    own_ref,
    tokens,
    dw_any,
    bias_any,
    seg_any,
    order_any,
    outer_rows_any,
    inner_rows_any,
    outer_cols_any,
    inner_cols_any,
    expand_any,
    project_any,
    out_ref,
    dw_ref,
    bias_ref,
    seg_ref,
    order_ref,
    outer_rows,
    inner_rows,
    outer_cols,
    inner_cols,
    expand_ref,
    project_ref,
    sems,
    sides,
    side_vals,
    taps,
    edge_cols,
    edge_rows,
    mixed,
    total,
):
    rows, steps, _, hidden = own_ref.shape
    cols = steps * SEG
    pairs = [
        (outer_rows_any.at[frame], outer_rows),
        (inner_rows_any.at[frame], inner_rows),
        (outer_cols_any.at[frame], outer_cols),
        (inner_cols_any.at[frame], inner_cols),
        (seg_any, seg_ref),
        (expand_any, expand_ref),
        (dw_any, dw_ref),
        (bias_any, bias_ref),
        (project_any, project_ref),
        (order_any, order_ref),
    ]
    copies = [pltpu.make_async_copy(src, dst, sems.at[i]) for i, (src, dst) in enumerate(pairs)]
    for copy in copies:
        copy.start()
    sides[...] = jnp.zeros_like(sides)
    for copy in copies[0:5]:
        copy.wait()
    even_row, even_col = even_ref[0] == 1, even_ref[1] == 1
    outer, inner = outer_rows[...], inner_rows[...]
    top, bottom = jnp.where(even_row, outer, inner), jnp.where(even_row, inner, outer)
    outer, inner = outer_cols[...], inner_cols[...]
    left, right = jnp.where(even_col, outer, inner), jnp.where(even_col, inner, outer)
    seg_one = seg_ref[:cols, :cols]
    top_tokens = dot(seg_one, top[0:cols]).astype(BF16)
    bottom_tokens = dot(seg_one, bottom[0:cols]).astype(BF16)
    top = 0.5 * top[cols : cols + 16].astype(F32)
    bottom = 0.5 * bottom[cols : cols + 16].astype(F32)
    sides[0:1] = top[0:1]
    sides[1 : rows + 1] = 0.5 * left.astype(F32)
    sides[rows + 1 : rows + 2] = bottom[0:1]
    sides[24:25] = top[1:2]
    sides[25 : rows + 25] = 0.5 * right.astype(F32)
    sides[rows + 25 : rows + 26] = bottom[1:2]
    halo = jnp.concatenate([top_tokens, bottom_tokens, sides[...].astype(BF16)], axis=0)
    place = lax.broadcasted_iota(jnp.int32, (SEG, CHUNK), 0)
    for copy in copies[5:8]:
        copy.wait()
    for i in range(3):
        taps[3 * i : 3 * i + 3] = 0.5 * dw_ref[i]
    taps[9:10] = 0.5 * bias_ref[...].reshape(1, hidden)

    def expand_halo(c):
        lanes = slice(c * CHUNK, (c + 1) * CHUNK)
        value = half_gelu(dot(halo, expand_ref[:, lanes]))
        edge_rows[:, :, :, lanes] = value[: 2 * cols].reshape(2, steps, SEG, CHUNK)
        side_vals[:, lanes] = value[2 * cols :]

    def plain(r, t, lanes):
        if r == 0:
            return edge_rows[0, t, :, lanes]
        if r == rows + 1:
            return edge_rows[1, t, :, lanes]
        return own_ref[r - 1, t, :, lanes]

    def fill_edges(c, r):
        lanes = slice(c * CHUNK, (c + 1) * CHUNK)
        before = pltpu.roll(plain(r, steps - 1, lanes), 1, 0)
        edge_cols[r, 0, :, lanes] = jnp.where(place == 0, side_vals[r : r + 1, lanes], before)
        after = pltpu.roll(plain(r, 0, lanes), SEG - 1, 0)
        edge_cols[r, 1, :, lanes] = jnp.where(place == SEG - 1, side_vals[24 + r : 25 + r, lanes], after)

    def conv_row(c, r):
        for lt in range(CHUNK // 128):
            lanes = slice(c * CHUNK + lt * 128, c * CHUNK + (lt + 1) * 128)
            acc = jnp.broadcast_to(taps[9:10, lanes].reshape(1, 1, 128), (steps, SEG, 128))
            for i in range(3):
                if r + i == 0:
                    middle = edge_rows[0, :, :, lanes]
                elif r + i == rows + 1:
                    middle = edge_rows[1, :, :, lanes]
                else:
                    middle = own_ref[r + i - 1, :, :, lanes]
                window = jnp.concatenate(
                    [edge_cols[r + i, 0:1, :, lanes], middle, edge_cols[r + i, 1:2, :, lanes]], axis=0
                )
                for j in range(3):
                    acc = acc + window[j : j + steps] * taps[3 * i + j : 3 * i + j + 1, lanes].reshape(1, 1, 128)
            mixed[r * cols : (r + 1) * cols, lanes] = half_gelu(acc).reshape(cols, 128).astype(BF16)

    def project_rows(c, start, stop):
        lanes = slice(c * CHUNK, (c + 1) * CHUNK)
        span = slice(start * cols, stop * cols)
        branch = dot(mixed[span, lanes], project_ref[lanes])
        total[span] = branch if c == 0 else total[span] + branch

    part = rows // 2
    for c in range(hidden // CHUNK):
        expand_halo(c)
        if c == 0:
            copies[8].wait()
            copies[9].wait()
        fill_edges(c, 0)
        fill_edges(c, 1)
        for r in range(rows):
            fill_edges(c, r + 2)
            conv_row(c, r)
            if r % part == part - 1 and r >= part:
                project_rows(c, r + 1 - 2 * part, r + 1 - part)
        project_rows(c, rows - part, rows)

    flag = keep_ref[frame, 0].astype(F32)
    span = order_ref.shape[0]
    groups = span // cols
    stride = rows // groups
    order = order_ref[...]
    for d in range(stride):
        parts = []
        for g in range(groups):
            r = g * stride + d
            residual = 2.0 * tokens[r * cols : (r + 1) * cols].astype(F32)
            parts.append((residual + flag * total[r * cols : (r + 1) * cols]).astype(BF16))
        value = parts[0] if groups == 1 else jnp.concatenate(parts, axis=0)
        out_ref[d * span : (d + 1) * span] = dot(order, value).astype(BF16)


def conv_call(frame, keep, even, own, tokens, dw, bias, seg, order, halo, expand_weight, project_weight):
    rows, steps, _, hidden = own.shape
    cols = steps * SEG
    channels = tokens.shape[1]
    large = [dw, bias, seg, order, *halo, expand_weight, project_weight]

    def body(*refs):
        conv_kernel(frame, *refs)

    def buffer(a, k):
        return pltpu.VMEM(a.shape[1:] if 4 <= k < 8 else a.shape, a.dtype)

    return pl.pallas_call(
        body,
        in_specs=[pl.BlockSpec(memory_space=pltpu.SMEM)] * 2
        + [pl.BlockSpec(memory_space=pltpu.VMEM)] * 2
        + [pl.BlockSpec(memory_space=pl.ANY)] * len(large),
        out_specs=pl.BlockSpec(memory_space=pltpu.VMEM),
        out_shape=jax.ShapeDtypeStruct((rows * cols, channels), BF16),
        scratch_shapes=[buffer(a, k) for k, a in enumerate(large)]
        + [
            pltpu.SemaphoreType.DMA((len(large),)),
            pltpu.VMEM((48, channels), F32),
            pltpu.VMEM((48, hidden), F32),
            pltpu.VMEM((16, hidden), F32),
            pltpu.VMEM((rows + 2, 2, SEG, hidden), F32),
            pltpu.VMEM((2, steps, SEG, hidden), F32),
            pltpu.VMEM((rows * cols, hidden), BF16),
            pltpu.VMEM((rows * cols, channels), F32),
        ],
        compiler_params=pltpu.CompilerParams(vmem_limit_bytes=32 * MIB),
        cost_estimate=pl.CostEstimate(flops=4 * 10**9, bytes_accessed=4 * 10**6, transcendentals=2 * 10**6),
    )(keep, even, own, tokens, *large)


def window_kernel(frame, keep_ref, x_ref, qkv_ref, out_w_ref, in_ref, down_ref, out_ref, held):
    windows = held.shape[1]
    sources, _, group, channels = held.shape
    count = sources * group
    head_dim = channels // HEADS
    per_tile = 128 // head_dim
    scale = head_dim ** (-0.5) * math.log2(math.e)
    held[...] = x_ref[...].astype(F32).reshape(held.shape)
    attend_flag = keep_ref[frame, 1].astype(F32)
    mlp_flag = keep_ref[frame, 2].astype(F32)
    head_of_lane = lax.broadcasted_iota(jnp.int32, (1, 128), 1) // head_dim
    ones = jnp.ones((count, 128), BF16)
    none = jnp.zeros((), BF16)

    def attend(residual):
        qkv = dot(normalize(residual).astype(BF16), qkv_ref[...]).astype(BF16)
        tiles = []
        for t in range(channels // 128):
            queries = qkv[:, t * 128 : (t + 1) * 128]
            keys_part = qkv[:, channels + t * 128 : channels + (t + 1) * 128]
            values_part = qkv[:, 2 * channels + t * 128 : 2 * channels + (t + 1) * 128]
            values_part = jnp.concatenate([values_part, ones], axis=1)
            tile = None
            for i in range(per_tile):
                scores = dot_t(jnp.where(head_of_lane == i, queries, none), keys_part)
                top_score = jnp.max(scores, axis=1, keepdims=True)
                weights = jnp.exp2((scores - top_score) * scale).astype(BF16)
                both = dot(weights, values_part)
                share = both[:, :128] * (1.0 / both[:, 128:])
                tile = share if tile is None else jnp.where(head_of_lane == i, share, tile)
            tiles.append(tile.astype(BF16))
        update = dot(jnp.concatenate(tiles, axis=1), out_w_ref[...])
        return (residual + attend_flag * update).astype(BF16).astype(F32)

    def mlp(residual):
        inner = gelu(dot(normalize(residual).astype(BF16), in_ref[...])).astype(BF16)
        return residual + mlp_flag * dot(inner, down_ref[...])

    def one_window(w, _):
        second = attend(held[:, w].reshape(count, channels))
        held[:, w] = mlp(second).reshape(sources, group, channels)
        return 0

    lax.fori_loop(0, windows, one_window, 0)
    out_ref[...] = held[...].reshape(out_ref.shape).astype(BF16)


def window_call(frame, keep, x, windows, group, qkv_weight, out_weight, mlp_in, mlp_out):
    tokens, channels = x.shape
    held = (tokens // (windows * group), windows, group, channels)

    def body(*refs):
        window_kernel(frame, *refs)

    return pl.pallas_call(
        body,
        in_specs=[pl.BlockSpec(memory_space=pltpu.SMEM)] + [pl.BlockSpec(memory_space=pltpu.VMEM)] * 5,
        out_specs=pl.BlockSpec(memory_space=pltpu.VMEM),
        out_shape=jax.ShapeDtypeStruct(x.shape, BF16),
        scratch_shapes=[pltpu.VMEM(held, F32)],
        compiler_params=pltpu.CompilerParams(vmem_limit_bytes=40 * MIB),
        cost_estimate=pl.CostEstimate(flops=9 * 10**9, bytes_accessed=4 * 10**6, transcendentals=6 * 10**6),
    )(keep, x, qkv_weight, out_weight, mlp_in, mlp_out)


def restore_kernel(x_ref, order_ref, *rest):
    out_ref = rest[-1]
    _, rows, cols, channels = out_ref.shape
    span = order_ref.shape[0]
    groups = span // cols
    stride = rows // groups
    order = order_ref[...]
    for d in range(stride):
        back = dot(order, x_ref[d * span : (d + 1) * span]).astype(BF16)
        for g in range(groups):
            out_ref[0, g * stride + d] = back[g * cols : (g + 1) * cols]


def restore_call(frame, x, order, out_shape, previous):
    _, rows, cols, channels = out_shape

    def whole(a):
        return pl.BlockSpec(a.shape, lambda i, n=a.ndim: (0,) * n)

    args = [x, order]
    specs = [whole(a) for a in args]
    aliases = {}
    if previous is not None:
        aliases = {len(args): 0}
        args.append(previous)
        specs.append(pl.BlockSpec(memory_space=pl.ANY))
    return pl.pallas_call(
        restore_kernel,
        grid=(1,),
        in_specs=specs,
        out_specs=pl.BlockSpec((1, rows, cols, channels), lambda i: (frame, 0, 0, 0)),
        out_shape=jax.ShapeDtypeStruct(out_shape, BF16),
        input_output_aliases=aliases,
        compiler_params=pltpu.CompilerParams(vmem_limit_bytes=16 * MIB),
        cost_estimate=pl.CostEstimate(flops=10**8, bytes_accessed=2 * 10**6, transcendentals=0),
    )(*args)


def neighbours(first, last, axis):
    size = lax.axis_size(axis)
    even = lax.axis_index(axis) % 2 == 0
    inner = [(i, i ^ 1) for i in range(size)]
    outer = [(i, i + 1) for i in range(1, size - 1, 2)]
    outer = outer + [(j, i) for i, j in outer]
    across = lax.ppermute(jnp.where(even, first, last), axis, outer)
    within = lax.ppermute(jnp.where(even, last, first), axis, inner)
    return even, across, within


def body(
    frames,
    keep,
    expand_weight,
    dw_kernel,
    conv_bias,
    project_weight,
    qkv_weight,
    out_weight,
    mlp_in,
    mlp_out,
):
    frame_count, rows, cols, channels = frames.shape
    rows_axis = lax.axis_size("ha")
    cols_axis = lax.axis_size("wa")
    row_stride = rows * rows_axis // GRID
    col_stride = cols * cols_axis // GRID
    assert row_stride == rows_axis and col_stride % cols_axis == 0
    cols_each = col_stride // cols_axis
    row_groups = rows // row_stride
    col_groups = cols // col_stride
    group = row_groups * col_groups
    devices = rows_axis * cols_axis

    even_col, outer_cols, inner_cols = neighbours(frames[:, :, 0], frames[:, :, cols - 1], "wa")
    left = jnp.where(even_col, outer_cols, inner_cols)
    right = jnp.where(even_col, inner_cols, outer_cols)

    def edge(r):
        spare = jnp.zeros((frame_count, 14, channels), BF16)
        return jnp.concatenate([frames[:, r], left[:, r : r + 1], right[:, r : r + 1], spare], axis=1)

    even_row, outer_rows, inner_rows = neighbours(edge(0), edge(rows - 1), "ha")
    halo = (outer_rows, inner_rows, outer_cols, inner_cols)
    even = jnp.stack([even_row, even_col]).astype(jnp.int32)

    to_segments = segment_order(cols, 2)
    to_message = message_order(row_groups, cols, col_stride, cols_each)
    from_segments = np.kron(np.eye(row_groups), segment_order(cols, 1)).T
    seg = jnp.asarray(0.5 * to_segments, BF16)
    order = jnp.asarray(to_message @ from_segments, BF16)
    order_back = jnp.asarray(to_message.T, BF16)
    def exchange(x):
        message = x.reshape(devices, -1, channels)
        return lax.all_to_all(message, ("ha", "wa"), split_axis=0, concat_axis=0, tiled=True).reshape(-1, channels)

    sent = []
    for f in range(frame_count):
        own, tokens = expand_call(f, seg, frames, expand_weight)
        first = conv_call(
            f, keep, even, own, tokens, dw_kernel, conv_bias, seg, order, halo, expand_weight, project_weight
        )
        sent.append(exchange(first))
    back = []
    for f in range(frame_count):
        x = sent[f]
        if group != 8:
            x = x.reshape(devices, cols_each, group, channels).swapaxes(0, 1).reshape(cols_each, -1, 8, channels)
            x = x.swapaxes(0, 1).reshape(-1, channels)
        x = window_call(f, keep, x, cols_each, 8, qkv_weight, out_weight, mlp_in, mlp_out)
        if group != 8:
            x = x.reshape(-1, cols_each, 8, channels).swapaxes(0, 1).reshape(cols_each, devices, group, channels)
            x = x.swapaxes(0, 1).reshape(-1, channels)
        back.append(exchange(x))
    result = None
    for f in range(frame_count):
        result = restore_call(f, back[f], order_back, frames.shape, result)
    return result


def solution(mesh):
    in_specs = (P(None, "ha", "wa", None), P(), P(), P(), P(), P(), P(), P(), P(), P())
    out_specs = P(None, "ha", "wa", None)
    return jax.shard_map(body, mesh=mesh, in_specs=in_specs, out_specs=out_specs, check_vma=False)
```

profile of v0, /device:TPU:1, one launch (start us, length us, event | category | flops | bytes accessed | tf_op | source)
XLA Modules:
  0.0 127.9 jit_solution(15775512879892704600)
XLA Ops:
  0.0 1.1 fusion
  1.1 0.7 collective-permute-start
  1.8 4.7 %collective-permute-start.1 = (bf16[2,16,384]{2,1,0:T(8,128)(2,1)S(1)}, bf16[2,16,384]{2,1,0:T(8,128)(2,1)S(1)}, u32[]{:S(2)}, u32[]{:S(2)}) collective-permute-start(bf16[2,16,384]{2,1,0:T(8,128)(2,1)S(1)} %get-tuple-element.20), channel_id=1, source_target_pairs={{0,1},{1,0},{2,3},{3,2},{4,5},{5,4},{6,7},{7,6},{8,9},{9,8},{10,11... | collective-permute-start | bytes 73736 | tf_op jit(solution)/shard_map/ppermute | solution.py:418
  6.5 1.0 slice_bitcast_fusion.1
  7.5 0.1 pad.7.clone
  7.6 0.0 collective-permute-done.refs_10_
  7.6 0.1 collective-permute-done.1.refs_11_
  7.8 0.1 broadcast_select_fusion
  7.9 1.9 %collective-permute-start.3 = (bf16[2,80,384]{2,1,0:T(8,128)(2,1)S(1)}, bf16[2,80,384]{2,1,0:T(8,128)(2,1)S(1)}, u32[]{:S(2)}, u32[]{:S(2)}) collective-permute-start(bf16[2,80,384]{2,1,0:T(8,128)(2,1)S(1)} %get-tuple-element.17), channel_id=1, source_target_pairs={{0,4},{4,0},{8,12},{12,8},{16,20},{20,16},{24,28},{28,24},{1,5},{5... | collective-permute-start | bytes 368648 | tf_op jit(solution)/shard_map/ppermute | solution.py:418
  9.8 3.0 %collective-permute-start.2 = (bf16[2,80,384]{2,1,0:T(8,128)(2,1)S(1)}, bf16[2,80,384]{2,1,0:T(8,128)(2,1)S(1)}, u32[]{:S(2)}, u32[]{:S(2)}) collective-permute-start(bf16[2,80,384]{2,1,0:T(8,128)(2,1)S(1)} %get-tuple-element.18), channel_id=1, source_target_pairs={{4,8},{12,16},{20,24},{8,4},{16,12},{24,20},{5,9},{13,17},{21,25},... | collective-permute-start | bytes 368648 | tf_op jit(solution)/shard_map/ppermute | solution.py:417
  12.8 0.0 copy-start.1
  12.8 1.4 %copy-done.1 = bf16[2,16,64,384]{3,2,1,0:T(8,128)(2,1)S(1)} copy-done((bf16[2,16,64,384]{3,2,1,0:T(8,128)(2,1)S(1)}, bf16[2,16,64,384]{3,2,1,0:T(8,128)(2,1)}, u32[]{:S(2)}) %copy-start.1) | copy-done | bytes 1572888
  14.2 0.0 copy-start.3
  14.2 1.3 copy-done.3
  15.5 0.0 copy-start.18
  15.5 0.8 copy-done.18
  16.3 0.0 copy-start.4
  16.3 0.0 copy-start.7
  16.3 0.0 copy-start.17
  16.3 0.0 copy-start.19
  16.3 0.0 copy-start.20
  16.3 2.6 %shard_map.130 = (f32[16,8,8,1536]{3,2,1,0:T(8,128)S(1)}, bf16[1024,384]{1,0:T(8,128)(2,1)S(1)}) custom-call(bf16[128,128]{1,0:T(8,128)(2,1)S(1)} %copy-done.18, bf16[2,16,64,384]{3,2,1,0:T(8,128)(2,1)S(1)} %copy-done.1, bf16[384,1536]{1,0:T(8,128)(2,1)S(1)} %copy-done.3), custom_call_target="tpu_custom_call" | custom-call | flops 3000000000 | bytes 4000000 | tf_op jit(solution)/shard_map/pallas_call | solution.py:100
  18.9 0.1 add_convert_fusion.refs_1_
  19.0 0.0 collective-permute-done.3.refs_9_
  19.0 0.0 collective-permute-done.2.refs_8_
  19.0 0.0 copy-done.4
  19.0 0.0 copy-done.7
  19.0 0.0 copy-done.15
  19.0 0.0 copy-done.16
  19.1 0.0 copy-done.17
  19.1 0.0 copy-done.19
  19.1 0.0 copy-done.20
  19.1 11.2 %shard_map.131 = bf16[1024,384]{1,0:T(8,128)(2,1)} custom-call(s32[2,3]{1,0:T(2,128)S(1)} %copy-done.17, s32[2]{0:T(128)S(1)} %add_convert_fusion.refs_1_, f32[16,8,8,1536]{3,2,1,0:T(8,128)S(1)} %get-tuple-element.11.refs_2_, bf16[1024,384]{1,0:T(8,128)(2,1)S(1)} %get-tuple-element.12.refs_3_, f32[3,3,1536]{2,1,0:T(4,128)S(1)} %copy-done.15, ...), custom_call_target="tpu_custom_call" | custom-call | flops 4000000000 | bytes 4000000 | tf_op jit(solution)/shard_map/pallas_call | solution.py:285
  30.3 0.0 copy-start.2
  30.3 3.6 %all-to-all-start.2 = ((bf16[32,32,384]{2,1,0:T(8,128)(2,1)}), bf16[32,32,384]{2,1,0:T(8,128)(2,1)S(1)}, u32[]{:S(2)}, u32[]{:S(2)}) async-start(bf16[32,32,384]{2,1,0:T(8,128)(2,1)} %bitcast.10), calls=%async_computation.2 | async-start | bytes 1572864 | tf_op jit(solution)/shard_map/all_to_all | solution.py:466
  33.8 0.0 copy-done.2
  33.8 0.0 copy-start.5
  33.9 1.3 copy-done.5
  35.1 2.6 %shard_map.127 = (f32[16,8,8,1536]{3,2,1,0:T(8,128)S(1)}, bf16[1024,384]{1,0:T(8,128)(2,1)S(1)}) custom-call(bf16[128,128]{1,0:T(8,128)(2,1)S(1)} %copy-done.19, bf16[2,16,64,384]{3,2,1,0:T(8,128)(2,1)S(1)} %copy-done.2, bf16[384,1536]{1,0:T(8,128)(2,1)S(1)} %copy-done.5), custom_call_target="tpu_custom_call" | custom-call | flops 3000000000 | bytes 4000000 | tf_op jit(solution)/shard_map/pallas_call | solution.py:100
  37.7 0.0 copy-done.6
  37.7 0.0 copy-done.8
  37.7 11.1 %shard_map.128 = bf16[1024,384]{1,0:T(8,128)(2,1)} custom-call(s32[2,3]{1,0:T(2,128)S(1)} %copy-done.17, s32[2]{0:T(128)S(1)} %add_convert_fusion.refs_1_, f32[16,8,8,1536]{3,2,1,0:T(8,128)S(1)} %get-tuple-element.9.refs_2_, bf16[1024,384]{1,0:T(8,128)(2,1)S(1)} %get-tuple-element.10.refs_3_, f32[3,3,1536]{2,1,0:T(4,128)S(1)} %copy-done.15, ...), custom_call_target="tpu_custom_call" | custom-call | flops 4000000000 | bytes 4000000 | tf_op jit(solution)/shard_map/pallas_call | solution.py:285
  48.9 0.0 copy-start.9
  48.9 0.0 copy-start.14
  48.9 5.7 %all-to-all-done.2 = bf16[32,32,384]{2,1,0:T(8,128)(2,1)S(1)} async-done(((bf16[32,32,384]{2,1,0:T(8,128)(2,1)}), bf16[32,32,384]{2,1,0:T(8,128)(2,1)S(1)}, u32[]{:S(2)}, u32[]{:S(2)}) %all-to-all-start.2) | async-done | bytes 786464 | tf_op jit(solution)/shard_map/all_to_all | solution.py:466
  54.6 3.2 %all-to-all-start = ((bf16[32,32,384]{2,1,0:T(8,128)(2,1)}), bf16[32,32,384]{2,1,0:T(8,128)(2,1)S(1)}, u32[]{:S(2)}, u32[]{:S(2)}) async-start(bf16[32,32,384]{2,1,0:T(8,128)(2,1)} %bitcast.6), calls=%async_computation | async-start | bytes 1572864 | tf_op jit(solution)/shard_map/all_to_all | solution.py:466
  57.8 0.0 copy-done.9
  57.8 0.0 copy-done.14
  57.8 0.0 copy-start.10
  57.9 1.3 copy-done.10
  59.1 1.2 copy-done.12
  60.3 13.8 %shard_map.132 = bf16[1024,384]{1,0:T(8,128)(2,1)} custom-call(s32[2,3]{1,0:T(2,128)S(1)} %copy-done.17, bf16[1024,384]{1,0:T(8,128)(2,1)S(1)} %bitcast.24, bf16[384,1152]{1,0:T(8,128)(2,1)S(1)} %copy-done.12, bf16[384,384]{1,0:T(8,128)(2,1)S(1)} %copy-done.14, bf16[384,1536]{1,0:T(8,128)(2,1)S(1)} %copy-done.9, bf16[1536,384]{1,0:T(8,128)(2,1)S(1)} %copy-done.10), custom_call_target="tpu_custom_call" | custom-call | flops 8999999488 | bytes 4000000 | tf_op jit(solution)/shard_map/pallas_call | solution.py:362
  74.1 4.6 %all-to-all-done = bf16[32,32,384]{2,1,0:T(8,128)(2,1)S(1)} async-done(((bf16[32,32,384]{2,1,0:T(8,128)(2,1)}), bf16[32,32,384]{2,1,0:T(8,128)(2,1)S(1)}, u32[]{:S(2)}, u32[]{:S(2)}) %all-to-all-start) | async-done | bytes 786464 | tf_op jit(solution)/shard_map/all_to_all | solution.py:466
  78.6 3.2 %all-to-all-start.3 = ((bf16[32,32,384]{2,1,0:T(8,128)(2,1)}), bf16[32,32,384]{2,1,0:T(8,128)(2,1)S(1)}, u32[]{:S(2)}, u32[]{:S(2)}) async-start(bf16[32,32,384]{2,1,0:T(8,128)(2,1)} %bitcast.12), calls=%async_computation.3 | async-start | bytes 1572864 | tf_op jit(solution)/shard_map/all_to_all | solution.py:466
  81.8 0.0 copy-start.11
  81.8 1.3 copy-done.11
  83.1 1.2 copy-done.13
  84.2 13.8 %shard_map.129 = bf16[1024,384]{1,0:T(8,128)(2,1)} custom-call(s32[2,3]{1,0:T(2,128)S(1)} %copy-done.17, bf16[1024,384]{1,0:T(8,128)(2,1)S(1)} %bitcast.25, bf16[384,1152]{1,0:T(8,128)(2,1)S(1)} %copy-done.13, bf16[384,384]{1,0:T(8,128)(2,1)S(1)} %copy-done.14, bf16[384,1536]{1,0:T(8,128)(2,1)S(1)} %copy-done.9, bf16[1536,384]{1,0:T(8,128)(2,1)S(1)} %copy-done.11), custom_call_target="tpu_custom_call" | custom-call | flops 8999999488 | bytes 4000000 | tf_op jit(solution)/shard_map/pallas_call | solution.py:362
  98.0 4.6 %all-to-all-done.3 = bf16[32,32,384]{2,1,0:T(8,128)(2,1)S(1)} async-done(((bf16[32,32,384]{2,1,0:T(8,128)(2,1)}), bf16[32,32,384]{2,1,0:T(8,128)(2,1)S(1)}, u32[]{:S(2)}, u32[]{:S(2)}) %all-to-all-start.3) | async-done | bytes 786464 | tf_op jit(solution)/shard_map/all_to_all | solution.py:466
  102.6 3.2 %all-to-all-start.1 = ((bf16[32,32,384]{2,1,0:T(8,128)(2,1)}), bf16[32,32,384]{2,1,0:T(8,128)(2,1)S(1)}, u32[]{:S(2)}, u32[]{:S(2)}) async-start(bf16[32,32,384]{2,1,0:T(8,128)(2,1)} %bitcast.8), calls=%async_computation.1 | async-start | bytes 1572864 | tf_op jit(solution)/shard_map/all_to_all | solution.py:466
  105.8 0.0 copy-done
  105.8 1.2 shard_map.133.rest_0_
  107.0 19.6 %all-to-all-done.1 = bf16[32,32,384]{2,1,0:T(8,128)(2,1)S(1)} async-done(((bf16[32,32,384]{2,1,0:T(8,128)(2,1)}), bf16[32,32,384]{2,1,0:T(8,128)(2,1)S(1)}, u32[]{:S(2)}, u32[]{:S(2)}) %all-to-all-start.1) | async-done | bytes 786464 | tf_op jit(solution)/shard_map/all_to_all | solution.py:466
  126.6 1.2 shard_map.134
  (11 shorter events, 0.1 us)
Async XLA Ops:
  1.1 6.5 %collective-permute-start = (bf16[2,16,384]{2,1,0:T(8,128)(2,1)S(1)}, bf16[2,16,384]{2,1,0:T(8,128)(2,1)S(1)}, u32[]{:S(2)}, u32[]{:S(2)}) collective-permute-start(bf16[2,16,384]{2,1,0:T(8,128)(2,1)S(1)} %get-tuple-element.19), channel_id=1, source_target_pairs={{1,2},{2,1},{5,6},{6,5},{9,10},{10,9},{13,14},{14,13},{17,18},{18,... | collective-permute-start | bytes 73736 | tf_op jit(solution)/shard_map/ppermute | solution.py:417
  1.8 6.0 %collective-permute-start.1 = (bf16[2,16,384]{2,1,0:T(8,128)(2,1)S(1)}, bf16[2,16,384]{2,1,0:T(8,128)(2,1)S(1)}, u32[]{:S(2)}, u32[]{:S(2)}) collective-permute-start(bf16[2,16,384]{2,1,0:T(8,128)(2,1)S(1)} %get-tuple-element.20), channel_id=1, source_target_pairs={{0,1},{1,0},{2,3},{3,2},{4,5},{5,4},{6,7},{7,6},{8,9},{9,8},{10,11... | collective-permute-start | bytes 73736 | tf_op jit(solution)/shard_map/ppermute | solution.py:418
  7.9 11.1 %collective-permute-start.3 = (bf16[2,80,384]{2,1,0:T(8,128)(2,1)S(1)}, bf16[2,80,384]{2,1,0:T(8,128)(2,1)S(1)}, u32[]{:S(2)}, u32[]{:S(2)}) collective-permute-start(bf16[2,80,384]{2,1,0:T(8,128)(2,1)S(1)} %get-tuple-element.17), channel_id=1, source_target_pairs={{0,4},{4,0},{8,12},{12,8},{16,20},{20,16},{24,28},{28,24},{1,5},{5... | collective-permute-start | bytes 368648 | tf_op jit(solution)/shard_map/ppermute | solution.py:418
  9.8 9.2 %collective-permute-start.2 = (bf16[2,80,384]{2,1,0:T(8,128)(2,1)S(1)}, bf16[2,80,384]{2,1,0:T(8,128)(2,1)S(1)}, u32[]{:S(2)}, u32[]{:S(2)}) collective-permute-start(bf16[2,80,384]{2,1,0:T(8,128)(2,1)S(1)} %get-tuple-element.18), channel_id=1, source_target_pairs={{4,8},{12,16},{20,24},{8,4},{16,12},{24,20},{5,9},{13,17},{21,25},... | collective-permute-start | bytes 368648 | tf_op jit(solution)/shard_map/ppermute | solution.py:417
  12.8 1.4 %copy-start.1 = (bf16[2,16,64,384]{3,2,1,0:T(8,128)(2,1)S(1)}, bf16[2,16,64,384]{3,2,1,0:T(8,128)(2,1)}, u32[]{:S(2)}) copy-start(bf16[2,16,64,384]{3,2,1,0:T(8,128)(2,1)} %refs_1_.3) | copy-start | bytes 4718596
  14.2 1.3 copy-start.3
  15.5 0.8 copy-start.18
  16.3 2.8 %copy-start.4 = (bf16[384,1536]{1,0:T(8,128)(2,1)S(1)}, bf16[384,1536]{1,0:T(8,128)(2,1)}, u32[]{:S(2)}) copy-start(bf16[384,1536]{1,0:T(8,128)(2,1)} %refs_12_.3) | copy-start | bytes 3538948
  16.3 2.8 %copy-start.7 = (bf16[1536,384]{1,0:T(8,128)(2,1)S(1)}, bf16[1536,384]{1,0:T(8,128)(2,1)}, u32[]{:S(2)}) copy-start(bf16[1536,384]{1,0:T(8,128)(2,1)} %refs_13_.3) | copy-start | bytes 3538948
  16.3 2.8 %copy-start.15 = (f32[3,3,1536]{2,1,0:T(4,128)S(1)}, f32[3,3,1536]{2,1,0:T(4,128)}, u32[]{:S(2)}) copy-start(f32[3,3,1536]{2,1,0:T(4,128)} %refs_4_.6) | copy-start | bytes 165892
  16.3 2.8 %copy-start.16 = (f32[1536]{0:T(1024)S(1)}, f32[1536]{0:T(1024)}, u32[]{:S(2)}) copy-start(f32[1536]{0:T(1024)} %refs_5_.6) | copy-start | bytes 18436
  16.3 2.8 %copy-start.17 = (s32[2,3]{1,0:T(2,128)S(1)}, s32[2,3]{1,0:T(2,128)}, u32[]{:S(2)}) copy-start(s32[2,3]{1,0:T(2,128)} %refs_0_.9) | copy-start | bytes 76
  16.3 2.8 %copy-start.19 = (bf16[128,128]{1,0:T(8,128)(2,1)S(1)}, bf16[128,128]{1,0:T(8,128)(2,1)}, u32[]{:S(2)}) copy-start(bf16[128,128]{1,0:T(8,128)(2,1)} %constant.35.clone.refs_0_.refs_6_) | copy-start | bytes 98308
  16.3 2.8 %copy-start.20 = (bf16[128,128]{1,0:T(8,128)(2,1)S(1)}, bf16[128,128]{1,0:T(8,128)(2,1)}, u32[]{:S(2)}) copy-start(bf16[128,128]{1,0:T(8,128)(2,1)} %constant.36.clone.refs_7_) | copy-start | bytes 98308
  30.3 3.6 %copy-start.2 = (bf16[2,16,64,384]{3,2,1,0:T(8,128)(2,1)S(1)}, bf16[2,16,64,384]{3,2,1,0:T(8,128)(2,1)}, u32[]{:S(2)}) copy-start(bf16[2,16,64,384]{3,2,1,0:T(8,128)(2,1)} %refs_1_.3) | copy-start | bytes 4718596
  30.3 24.4 %all-to-all-start.2 = ((bf16[32,32,384]{2,1,0:T(8,128)(2,1)}), bf16[32,32,384]{2,1,0:T(8,128)(2,1)S(1)}, u32[]{:S(2)}, u32[]{:S(2)}) async-start(bf16[32,32,384]{2,1,0:T(8,128)(2,1)} %bitcast.10), calls=%async_computation.2 | async-start | bytes 1572864 | tf_op jit(solution)/shard_map/all_to_all | solution.py:466
  33.8 1.3 copy-start.5
  35.1 2.6 %copy-start.6 = (bf16[384,1536]{1,0:T(8,128)(2,1)S(1)}, bf16[384,1536]{1,0:T(8,128)(2,1)}, u32[]{:S(2)}) copy-start(bf16[384,1536]{1,0:T(8,128)(2,1)} %refs_12_.3) | copy-start | bytes 3538948
  35.1 2.6 %copy-start.8 = (bf16[1536,384]{1,0:T(8,128)(2,1)S(1)}, bf16[1536,384]{1,0:T(8,128)(2,1)}, u32[]{:S(2)}) copy-start(bf16[1536,384]{1,0:T(8,128)(2,1)} %refs_13_.3) | copy-start | bytes 3538948
  48.9 8.9 %copy-start.9 = (bf16[384,1536]{1,0:T(8,128)(2,1)S(1)}, bf16[384,1536]{1,0:T(8,128)(2,1)}, u32[]{:S(2)}) copy-start(bf16[384,1536]{1,0:T(8,128)(2,1)} %refs_4_.7) | copy-start | bytes 3538948
  48.9 8.9 %copy-start.14 = (bf16[384,384]{1,0:T(8,128)(2,1)S(1)}, bf16[384,384]{1,0:T(8,128)(2,1)}, u32[]{:S(2)}) copy-start(bf16[384,384]{1,0:T(8,128)(2,1)} %refs_3_.3) | copy-start | bytes 884740
  54.6 24.0 %all-to-all-start = ((bf16[32,32,384]{2,1,0:T(8,128)(2,1)}), bf16[32,32,384]{2,1,0:T(8,128)(2,1)S(1)}, u32[]{:S(2)}, u32[]{:S(2)}) async-start(bf16[32,32,384]{2,1,0:T(8,128)(2,1)} %bitcast.6), calls=%async_computation | async-start | bytes 1572864 | tf_op jit(solution)/shard_map/all_to_all | solution.py:466
  57.8 1.3 copy-start.10
  59.1 1.2 copy-start.12
  78.6 24.0 %all-to-all-start.3 = ((bf16[32,32,384]{2,1,0:T(8,128)(2,1)}), bf16[32,32,384]{2,1,0:T(8,128)(2,1)S(1)}, u32[]{:S(2)}, u32[]{:S(2)}) async-start(bf16[32,32,384]{2,1,0:T(8,128)(2,1)} %bitcast.12), calls=%async_computation.3 | async-start | bytes 1572864 | tf_op jit(solution)/shard_map/all_to_all | solution.py:466
  81.8 1.3 copy-start.11
  83.1 1.2 copy-start.13
  98.0 7.8 %copy-start = (bf16[128,128]{1,0:T(8,128)(2,1)S(1)}, bf16[128,128]{1,0:T(8,128)(2,1)}, u32[]{:S(2)}) copy-start(bf16[128,128]{1,0:T(8,128)(2,1)} %constant.37.clone.order_ref) | copy-start | bytes 98308
  102.6 24.0 %all-to-all-start.1 = ((bf16[32,32,384]{2,1,0:T(8,128)(2,1)}), bf16[32,32,384]{2,1,0:T(8,128)(2,1)S(1)}, u32[]{:S(2)}, u32[]{:S(2)}) async-start(bf16[32,32,384]{2,1,0:T(8,128)(2,1)} %bitcast.8), calls=%async_computation.1 | async-start | bytes 1572864 | tf_op jit(solution)/shard_map/all_to_all | solution.py:466
where the time goes:
time: 129 us; the launch traced here: 128 us
  Pallas kernels  57.5 us (45%)
  waiting for transfers between devices  34.7 us (27%)
  starting transfers between devices  23.3 us (18%)
  local copies, waits for them, and re-layouts  11.8 us (9%)
    all_to_all x4, waiting for transfers between devices, exchange(): lax.all_to_all(message, ('ha', 'wa'), split_axis=0, concat_axis=0, tiled=...  34.5 us
    pallas_call x2, Pallas kernels, window_call(): pl.pallas_call(body, in_specs=[pl.BlockSpec(memory_space=pltpu.SMEM)] + [...  27.5 us
    pallas_call x2, Pallas kernels, conv_call(): pl.pallas_call(body, in_specs=[pl.BlockSpec(memory_space=pltpu.SMEM)] * 2...  22.3 us
    all_to_all x4, starting transfers between devices, exchange(): lax.all_to_all(message, ('ha', 'wa'), split_axis=0, concat_axis=0, tiled=...  13 us
    unnamed x42, local copies, waits for them, and re-layouts  9.63 us
    ppermute x2, starting transfers between devices, neighbours(): within = lax.ppermute(jnp.where(even, last, first), axis, inner)  6.62 us
    pallas_call x2, Pallas kernels, expand_call(): pl.pallas_call(body, in_specs=[pl.BlockSpec(memory_space=pl.ANY)] * 3, ou...  5.2 us
    ppermute x2, starting transfers between devices, neighbours(): across = lax.ppermute(jnp.where(even, first, last), axis, outer)  3.68 us
  transfers between devices with their start and end apart: 8, of which 5 were waited for; matrix products, arithmetic and copies ran while one was open for 1% of the time, Pallas kernels for 35%

commit v1 on v0

--- a/solution.py
+++ b/solution.py
@@ -11,7 +11,7 @@
 HEADS = 12
 GRID = 16
 SEG = 8
-CHUNK = 768
+CHUNK = 1536
 F32 = jnp.float32
 BF16 = jnp.bfloat16
 MIB = 1024 * 1024
@@ -51,6 +51,15 @@
             for s in range(SEG):
                 matrix[row * cols + t * SEG + s, row * cols + s * steps + t] = 1
     return matrix
+
+
+def segments(cols, count):
+    steps = cols // SEG
+    shape = (count * cols, count * cols)
+    place = lax.broadcasted_iota(jnp.int32, shape, 0)
+    inside = place % cols
+    source = place - inside + inside % SEG * steps + inside // SEG
+    return jnp.where(lax.broadcasted_iota(jnp.int32, shape, 1) == source, 0.5, 0.0).astype(BF16)
 
 
 def message_order(row_groups, cols, col_stride, cols_each):
@@ -67,21 +76,15 @@
     return matrix
 
 
-def expand_kernel(frame, seg_any, x_any, expand_any, expanded, tokens, x_ref, expand_ref, seg_ref, sems):
+def expand_kernel(frame, x_ref, expand_ref, expanded, tokens):
     rows, steps, _, hidden = expanded.shape
     cols = steps * SEG
     channels = x_ref.shape[-1]
-    pairs = [(seg_any, seg_ref), (x_any.at[frame], x_ref), (expand_any, expand_ref)]
-    copies = [pltpu.make_async_copy(src, dst, sems.at[i]) for i, (src, dst) in enumerate(pairs)]
-    for copy in copies:
-        copy.start()
-    copies[0].wait()
-    copies[1].wait()
     pair = 2 * cols
+    seg = segments(cols, 2)
     for r in range(rows // 2):
-        both = x_ref[2 * r : 2 * r + 2].reshape(pair, channels)
-        tokens[r * pair : (r + 1) * pair] = dot(seg_ref[...], both).astype(BF16)
-    copies[2].wait()
+        both = x_ref[frame, 2 * r : 2 * r + 2].reshape(pair, channels)
+        tokens[r * pair : (r + 1) * pair] = dot(seg, both).astype(BF16)
     block = 4
     for c in range(hidden // CHUNK):
         lanes = slice(c * CHUNK, (c + 1) * CHUNK)
@@ -90,7 +93,7 @@
             expanded[r : r + block, :, :, lanes] = value.reshape(block, steps, SEG, CHUNK)
 
 
-def expand_call(frame, seg, x, expand_weight):
+def expand_call(frame, x, expand_weight):
     _, rows, cols, channels = x.shape
     hidden = expand_weight.shape[1]
 
@@ -99,21 +102,15 @@
 
     return pl.pallas_call(
         body,
-        in_specs=[pl.BlockSpec(memory_space=pl.ANY)] * 3,
+        in_specs=[pl.BlockSpec(memory_space=pltpu.VMEM)] * 2,
         out_specs=[pl.BlockSpec(memory_space=pltpu.VMEM)] * 2,
         out_shape=[
             jax.ShapeDtypeStruct((rows, cols // SEG, SEG, hidden), F32),
             jax.ShapeDtypeStruct((rows * cols, channels), BF16),
         ],
-        scratch_shapes=[
-            pltpu.VMEM(x.shape[1:], BF16),
-            pltpu.VMEM(expand_weight.shape, BF16),
-            pltpu.VMEM(seg.shape, BF16),
-            pltpu.SemaphoreType.DMA((3,)),
-        ],
         compiler_params=pltpu.CompilerParams(vmem_limit_bytes=24 * MIB),
         cost_estimate=pl.CostEstimate(flops=3 * 10**9, bytes_accessed=4 * 10**6, transcendentals=2 * 10**6),
-    )(seg, x, expand_weight)
+    )(x, expand_weight)
 
 
 def conv_kernel(
@@ -122,26 +119,23 @@
     even_ref,
     own_ref,
     tokens,
+    expand_ref,
     dw_any,
     bias_any,
-    seg_any,
     order_any,
     outer_rows_any,
     inner_rows_any,
     outer_cols_any,
     inner_cols_any,
-    expand_any,
     project_any,
     out_ref,
     dw_ref,
     bias_ref,
-    seg_ref,
     order_ref,
     outer_rows,
     inner_rows,
     outer_cols,
     inner_cols,
-    expand_ref,
     project_ref,
     sems,
     sides,
@@ -159,8 +153,6 @@
         (inner_rows_any.at[frame], inner_rows),
         (outer_cols_any.at[frame], outer_cols),
         (inner_cols_any.at[frame], inner_cols),
-        (seg_any, seg_ref),
-        (expand_any, expand_ref),
         (dw_any, dw_ref),
         (bias_any, bias_ref),
         (project_any, project_ref),
@@ -170,14 +162,14 @@
     for copy in copies:
         copy.start()
     sides[...] = jnp.zeros_like(sides)
-    for copy in copies[0:5]:
+    for copy in copies[0:4]:
         copy.wait()
     even_row, even_col = even_ref[0] == 1, even_ref[1] == 1
     outer, inner = outer_rows[...], inner_rows[...]
     top, bottom = jnp.where(even_row, outer, inner), jnp.where(even_row, inner, outer)
     outer, inner = outer_cols[...], inner_cols[...]
     left, right = jnp.where(even_col, outer, inner), jnp.where(even_col, inner, outer)
-    seg_one = seg_ref[:cols, :cols]
+    seg_one = segments(cols, 1)
     top_tokens = dot(seg_one, top[0:cols]).astype(BF16)
     bottom_tokens = dot(seg_one, bottom[0:cols]).astype(BF16)
     top = 0.5 * top[cols : cols + 16].astype(F32)
@@ -190,7 +182,7 @@
     sides[rows + 25 : rows + 26] = bottom[1:2]
     halo = jnp.concatenate([top_tokens, bottom_tokens, sides[...].astype(BF16)], axis=0)
     place = lax.broadcasted_iota(jnp.int32, (SEG, CHUNK), 0)
-    for copy in copies[5:8]:
+    for copy in copies[4:6]:
         copy.wait()
     for i in range(3):
         taps[3 * i : 3 * i + 3] = 0.5 * dw_ref[i]
@@ -217,6 +209,7 @@
         edge_cols[r, 1, :, lanes] = jnp.where(place == SEG - 1, side_vals[24 + r : 25 + r, lanes], after)
 
     def conv_row(c, r):
+        pieces = []
         for lt in range(CHUNK // 128):
             lanes = slice(c * CHUNK + lt * 128, c * CHUNK + (lt + 1) * 128)
             acc = jnp.broadcast_to(taps[9:10, lanes].reshape(1, 1, 128), (steps, SEG, 128))
@@ -232,28 +225,32 @@
                 )
                 for j in range(3):
                     acc = acc + window[j : j + steps] * taps[3 * i + j : 3 * i + j + 1, lanes].reshape(1, 1, 128)
-            mixed[r * cols : (r + 1) * cols, lanes] = half_gelu(acc).reshape(cols, 128).astype(BF16)
-
-    def project_rows(c, start, stop):
+            pieces.append(half_gelu(acc).reshape(cols, 128).astype(BF16))
+        return jnp.concatenate(pieces, axis=1)
+
+    def project_rows(c, start, stop, values):
         lanes = slice(c * CHUNK, (c + 1) * CHUNK)
         span = slice(start * cols, stop * cols)
-        branch = dot(mixed[span, lanes], project_ref[lanes])
+        branch = dot(jnp.concatenate(values, axis=0), project_ref[lanes])
         total[span] = branch if c == 0 else total[span] + branch
 
     part = rows // 2
     for c in range(hidden // CHUNK):
         expand_halo(c)
         if c == 0:
-            copies[8].wait()
-            copies[9].wait()
+            copies[6].wait()
+            copies[7].wait()
         fill_edges(c, 0)
         fill_edges(c, 1)
+        values, ready = [], None
         for r in range(rows):
             fill_edges(c, r + 2)
-            conv_row(c, r)
-            if r % part == part - 1 and r >= part:
-                project_rows(c, r + 1 - 2 * part, r + 1 - part)
-        project_rows(c, rows - part, rows)
+            values.append(conv_row(c, r))
+            if len(values) == part:
+                if ready is not None:
+                    project_rows(c, r + 1 - 2 * part, r + 1 - part, ready)
+                ready, values = values, []
+        project_rows(c, rows - part, rows, ready)
 
     flag = keep_ref[frame, 0].astype(F32)
     span = order_ref.shape[0]
@@ -270,22 +267,22 @@
         out_ref[d * span : (d + 1) * span] = dot(order, value).astype(BF16)
 
 
-def conv_call(frame, keep, even, own, tokens, dw, bias, seg, order, halo, expand_weight, project_weight):
+def conv_call(frame, keep, even, own, tokens, expand_weight, dw, bias, order, halo, project_weight):
     rows, steps, _, hidden = own.shape
     cols = steps * SEG
     channels = tokens.shape[1]
-    large = [dw, bias, seg, order, *halo, expand_weight, project_weight]
+    large = [dw, bias, order, *halo, project_weight]
 
     def body(*refs):
         conv_kernel(frame, *refs)
 
     def buffer(a, k):
-        return pltpu.VMEM(a.shape[1:] if 4 <= k < 8 else a.shape, a.dtype)
+        return pltpu.VMEM(a.shape[1:] if 3 <= k < 7 else a.shape, a.dtype)
 
     return pl.pallas_call(
         body,
         in_specs=[pl.BlockSpec(memory_space=pltpu.SMEM)] * 2
-        + [pl.BlockSpec(memory_space=pltpu.VMEM)] * 2
+        + [pl.BlockSpec(memory_space=pltpu.VMEM)] * 3
         + [pl.BlockSpec(memory_space=pl.ANY)] * len(large),
         out_specs=pl.BlockSpec(memory_space=pltpu.VMEM),
         out_shape=jax.ShapeDtypeStruct((rows * cols, channels), BF16),
@@ -302,7 +299,7 @@
         ],
         compiler_params=pltpu.CompilerParams(vmem_limit_bytes=32 * MIB),
         cost_estimate=pl.CostEstimate(flops=4 * 10**9, bytes_accessed=4 * 10**6, transcendentals=2 * 10**6),
-    )(keep, even, own, tokens, *large)
+    )(keep, even, own, tokens, expand_weight, *large)
 
 
 def window_kernel(frame, keep_ref, x_ref, qkv_ref, out_w_ref, in_ref, down_ref, out_ref, held):
@@ -455,10 +452,8 @@
     halo = (outer_rows, inner_rows, outer_cols, inner_cols)
     even = jnp.stack([even_row, even_col]).astype(jnp.int32)
 
-    to_segments = segment_order(cols, 2)
     to_message = message_order(row_groups, cols, col_stride, cols_each)
     from_segments = np.kron(np.eye(row_groups), segment_order(cols, 1)).T
-    seg = jnp.asarray(0.5 * to_segments, BF16)
     order = jnp.asarray(to_message @ from_segments, BF16)
     order_back = jnp.asarray(to_message.T, BF16)
     def exchange(x):
@@ -467,9 +462,9 @@
 
     sent = []
     for f in range(frame_count):
-        own, tokens = expand_call(f, seg, frames, expand_weight)
+        own, tokens = expand_call(f, frames, expand_weight)
         first = conv_call(
-            f, keep, even, own, tokens, dw_kernel, conv_bias, seg, order, halo, expand_weight, project_weight
+            f, keep, even, own, tokens, expand_weight, dw_kernel, conv_bias, order, halo, project_weight
         )
         sent.append(exchange(first))
     back = []

time: 129 us -> 126 us (0.977)
  Pallas kernels: 57.5 us -> 54.1 us
  waiting for transfers between devices: 34.7 us -> 36.3 us
    pallas_call x2, Pallas kernels: 22.3 us -> 19.9 us  [conv_call(): pl.pallas_call(body, in_specs=[pl.BlockSpec(memory_space=pltpu.SMEM)] * 2...]
    all_to_all x4, waiting for transfers between devices: 34.5 us -> 36.2 us  [exchange(): lax.all_to_all(message, ('ha', 'wa'), split_axis=0, concat_axis=0, tiled=...]
    unnamed x42 -> x38, local copies, waits for them, and re-layouts: 9.63 us -> 8.86 us
  transfers between devices with their start and end apart: 8 -> 8, of which waited for: 5 -> 5; matrix products, arithmetic and copies ran while one was open for 1% -> 1% of each run, Pallas kernels for 35% -> 34%
where the time goes in v1:
time: 126 us; the launch traced here: 125 us
  Pallas kernels  54.1 us (43%)
  waiting for transfers between devices  36.3 us (29%)
  starting transfers between devices  23.3 us (18%)
  local copies, waits for them, and re-layouts  11 us (9%)
    all_to_all x4, waiting for transfers between devices, exchange(): lax.all_to_all(message, ('ha', 'wa'), split_axis=0, concat_axis=0, tiled=...  36.2 us
    pallas_call x2, Pallas kernels, window_call(): pl.pallas_call(body, in_specs=[pl.BlockSpec(memory_space=pltpu.SMEM)] + [...  27.6 us
    pallas_call x2, Pallas kernels, conv_call(): pl.pallas_call(body, in_specs=[pl.BlockSpec(memory_space=pltpu.SMEM)] * 2...  19.9 us
    all_to_all x4, starting transfers between devices, exchange(): lax.all_to_all(message, ('ha', 'wa'), split_axis=0, concat_axis=0, tiled=...  13 us
    unnamed x38, local copies, waits for them, and re-layouts  8.86 us
    ppermute x2, starting transfers between devices, neighbours(): within = lax.ppermute(jnp.where(even, last, first), axis, inner)  6.62 us
    pallas_call x2, Pallas kernels, expand_call(): pl.pallas_call(body, in_specs=[pl.BlockSpec(memory_space=pltpu.VMEM)] * 2...  4.15 us
    ppermute x2, starting transfers between devices, neighbours(): across = lax.ppermute(jnp.where(even, first, last), axis, outer)  3.68 us
  transfers between devices with their start and end apart: 8, of which 5 were waited for; matrix products, arithmetic and copies ran while one was open for 1% of the time, Pallas kernels for 34%

profile of v1, /device:TPU:1, one launch (start us, length us, event | category | flops | bytes accessed | tf_op | source)
XLA Modules:
  0.0 125.4 jit_solution(6665938082186045664)
XLA Ops:
  0.0 1.1 fusion
  1.1 0.7 collective-permute-start
  1.8 4.7 %collective-permute-start.1 = (bf16[2,16,384]{2,1,0:T(8,128)(2,1)S(1)}, bf16[2,16,384]{2,1,0:T(8,128)(2,1)S(1)}, u32[]{:S(2)}, u32[]{:S(2)}) collective-permute-start(bf16[2,16,384]{2,1,0:T(8,128)(2,1)S(1)} %get-tuple-element.20), channel_id=1, source_target_pairs={{0,1},{1,0},{2,3},{3,2},{4,5},{5,4},{6,7},{7,6},{8,9},{9,8},{10,11... | collective-permute-start | bytes 73736 | tf_op jit(solution)/shard_map/ppermute | solution.py:415
  6.5 1.0 slice_bitcast_fusion.1
  7.5 0.1 pad.7.clone
  7.6 0.0 collective-permute-done.refs_10_
  7.6 0.1 collective-permute-done.1.refs_11_
  7.8 0.1 broadcast_select_fusion
  7.9 1.9 %collective-permute-start.3 = (bf16[2,80,384]{2,1,0:T(8,128)(2,1)S(1)}, bf16[2,80,384]{2,1,0:T(8,128)(2,1)S(1)}, u32[]{:S(2)}, u32[]{:S(2)}) collective-permute-start(bf16[2,80,384]{2,1,0:T(8,128)(2,1)S(1)} %get-tuple-element.17), channel_id=1, source_target_pairs={{0,4},{4,0},{8,12},{12,8},{16,20},{20,16},{24,28},{28,24},{1,5},{5... | collective-permute-start | bytes 368648 | tf_op jit(solution)/shard_map/ppermute | solution.py:415
  9.8 3.0 %collective-permute-start.2 = (bf16[2,80,384]{2,1,0:T(8,128)(2,1)S(1)}, bf16[2,80,384]{2,1,0:T(8,128)(2,1)S(1)}, u32[]{:S(2)}, u32[]{:S(2)}) collective-permute-start(bf16[2,80,384]{2,1,0:T(8,128)(2,1)S(1)} %get-tuple-element.18), channel_id=1, source_target_pairs={{4,8},{12,16},{20,24},{8,4},{16,12},{24,20},{5,9},{13,17},{21,25},... | collective-permute-start | bytes 368648 | tf_op jit(solution)/shard_map/ppermute | solution.py:414
  12.8 0.0 copy-start.1
  12.8 1.4 %copy-done.1 = bf16[2,16,64,384]{3,2,1,0:T(8,128)(2,1)S(1)} copy-done((bf16[2,16,64,384]{3,2,1,0:T(8,128)(2,1)S(1)}, bf16[2,16,64,384]{3,2,1,0:T(8,128)(2,1)}, u32[]{:S(2)}) %copy-start.1) | copy-done | bytes 1572888
  14.2 0.0 copy-start.3
  14.2 1.3 %copy-done.3 = bf16[384,1536]{1,0:T(8,128)(2,1)S(1)} copy-done((bf16[384,1536]{1,0:T(8,128)(2,1)S(1)}, bf16[384,1536]{1,0:T(8,128)(2,1)}, u32[]{:S(2)}) %copy-start.3) | copy-done | bytes 1179672
  15.5 0.0 copy-start.4
  15.5 0.0 copy-start.7
  15.5 0.0 copy-start.15
  15.5 0.0 copy-start.16
  15.5 0.0 copy-start.17
  15.5 0.0 copy-start.18
  15.6 2.1 %shard_map.121 = (f32[16,8,8,1536]{3,2,1,0:T(8,128)S(1)}, bf16[1024,384]{1,0:T(8,128)(2,1)S(1)}) custom-call(bf16[2,16,64,384]{3,2,1,0:T(8,128)(2,1)S(1)} %copy-done.1, bf16[384,1536]{1,0:T(8,128)(2,1)S(1)} %copy-done.3), custom_call_target="tpu_custom_call" | custom-call | flops 3000000000 | bytes 4000000 | tf_op jit(solution)/shard_map/pallas_call | solution.py:103
  17.6 0.1 add_convert_fusion.refs_1_
  17.7 0.0 collective-permute-done.3.refs_9_
  17.7 0.0 collective-permute-done.2.refs_8_
  17.7 0.0 copy-done.4
  17.7 0.0 copy-done.7
  17.7 0.0 copy-done.15
  17.7 0.0 copy-done.16
  17.8 0.0 copy-done.17
  17.8 0.0 copy-done.18
  17.8 10.0 %shard_map.122 = bf16[1024,384]{1,0:T(8,128)(2,1)} custom-call(s32[2,3]{1,0:T(2,128)S(1)} %copy-done.17, s32[2]{0:T(128)S(1)} %add_convert_fusion.refs_1_, f32[16,8,8,1536]{3,2,1,0:T(8,128)S(1)} %get-tuple-element.11.refs_2_, bf16[1024,384]{1,0:T(8,128)(2,1)S(1)} %get-tuple-element.12.refs_3_, bf16[384,1536]{1,0:T(8,128)(2,1)S(1)} %copy-done.4, ...), custom_call_target="tpu_custom_call" | custom-call | flops 4000000000 | bytes 4000000 | tf_op jit(solution)/shard_map/pallas_call | solution.py:282
  27.8 0.0 copy-start.2
  27.8 3.6 %all-to-all-start.2 = ((bf16[32,32,384]{2,1,0:T(8,128)(2,1)}), bf16[32,32,384]{2,1,0:T(8,128)(2,1)S(1)}, u32[]{:S(2)}, u32[]{:S(2)}) async-start(bf16[32,32,384]{2,1,0:T(8,128)(2,1)} %bitcast.10), calls=%async_computation.2 | async-start | bytes 1572864 | tf_op jit(solution)/shard_map/all_to_all | solution.py:461
  31.3 0.0 copy-done.2
  31.3 0.0 copy-start.5
  31.4 1.3 %copy-done.5 = bf16[384,1536]{1,0:T(8,128)(2,1)S(1)} copy-done((bf16[384,1536]{1,0:T(8,128)(2,1)S(1)}, bf16[384,1536]{1,0:T(8,128)(2,1)}, u32[]{:S(2)}) %copy-start.5) | copy-done | bytes 1179672
  32.6 0.0 copy-start.6
  32.6 0.0 copy-start.8
  32.6 2.1 %shard_map.118 = (f32[16,8,8,1536]{3,2,1,0:T(8,128)S(1)}, bf16[1024,384]{1,0:T(8,128)(2,1)S(1)}) custom-call(bf16[2,16,64,384]{3,2,1,0:T(8,128)(2,1)S(1)} %copy-done.2, bf16[384,1536]{1,0:T(8,128)(2,1)S(1)} %copy-done.5), custom_call_target="tpu_custom_call" | custom-call | flops 3000000000 | bytes 4000000 | tf_op jit(solution)/shard_map/pallas_call | solution.py:103
  34.7 0.0 copy-done.6
  34.7 0.0 copy-done.8
  34.7 9.9 %shard_map.119 = bf16[1024,384]{1,0:T(8,128)(2,1)} custom-call(s32[2,3]{1,0:T(2,128)S(1)} %copy-done.17, s32[2]{0:T(128)S(1)} %add_convert_fusion.refs_1_, f32[16,8,8,1536]{3,2,1,0:T(8,128)S(1)} %get-tuple-element.9.refs_2_, bf16[1024,384]{1,0:T(8,128)(2,1)S(1)} %get-tuple-element.10.refs_3_, bf16[384,1536]{1,0:T(8,128)(2,1)S(1)} %copy-done.6, ...), custom_call_target="tpu_custom_call" | custom-call | flops 4000000000 | bytes 4000000 | tf_op jit(solution)/shard_map/pallas_call | solution.py:282
  44.7 0.0 copy-start.9
  44.7 0.0 copy-start.14
  44.7 7.4 %all-to-all-done.2 = bf16[32,32,384]{2,1,0:T(8,128)(2,1)S(1)} async-done(((bf16[32,32,384]{2,1,0:T(8,128)(2,1)}), bf16[32,32,384]{2,1,0:T(8,128)(2,1)S(1)}, u32[]{:S(2)}, u32[]{:S(2)}) %all-to-all-start.2) | async-done | bytes 786464 | tf_op jit(solution)/shard_map/all_to_all | solution.py:461
  52.2 3.2 %all-to-all-start = ((bf16[32,32,384]{2,1,0:T(8,128)(2,1)}), bf16[32,32,384]{2,1,0:T(8,128)(2,1)S(1)}, u32[]{:S(2)}, u32[]{:S(2)}) async-start(bf16[32,32,384]{2,1,0:T(8,128)(2,1)} %bitcast.6), calls=%async_computation | async-start | bytes 1572864 | tf_op jit(solution)/shard_map/all_to_all | solution.py:461
  55.3 0.0 copy-done.9
  55.3 0.0 copy-done.14
  55.3 0.0 copy-start.10
  55.4 1.3 %copy-done.10 = bf16[1536,384]{1,0:T(8,128)(2,1)S(1)} copy-done((bf16[1536,384]{1,0:T(8,128)(2,1)S(1)}, bf16[1536,384]{1,0:T(8,128)(2,1)}, u32[]{:S(2)}) %copy-start.10) | copy-done | bytes 1179672
  56.6 1.2 copy-done.12
  57.8 13.8 %shard_map.123 = bf16[1024,384]{1,0:T(8,128)(2,1)} custom-call(s32[2,3]{1,0:T(2,128)S(1)} %copy-done.17, bf16[1024,384]{1,0:T(8,128)(2,1)S(1)} %bitcast.24, bf16[384,1152]{1,0:T(8,128)(2,1)S(1)} %copy-done.12, bf16[384,384]{1,0:T(8,128)(2,1)S(1)} %copy-done.14, bf16[384,1536]{1,0:T(8,128)(2,1)S(1)} %copy-done.9, bf16[1536,384]{1,0:T(8,128)(2,1)S(1)} %copy-done.10), custom_call_target="tpu_custom_call" | custom-call | flops 8999999488 | bytes 4000000 | tf_op jit(solution)/shard_map/pallas_call | solution.py:359
  71.6 4.6 %all-to-all-done = bf16[32,32,384]{2,1,0:T(8,128)(2,1)S(1)} async-done(((bf16[32,32,384]{2,1,0:T(8,128)(2,1)}), bf16[32,32,384]{2,1,0:T(8,128)(2,1)S(1)}, u32[]{:S(2)}, u32[]{:S(2)}) %all-to-all-start) | async-done | bytes 786464 | tf_op jit(solution)/shard_map/all_to_all | solution.py:461
  76.1 3.2 %all-to-all-start.3 = ((bf16[32,32,384]{2,1,0:T(8,128)(2,1)}), bf16[32,32,384]{2,1,0:T(8,128)(2,1)S(1)}, u32[]{:S(2)}, u32[]{:S(2)}) async-start(bf16[32,32,384]{2,1,0:T(8,128)(2,1)} %bitcast.12), calls=%async_computation.3 | async-start | bytes 1572864 | tf_op jit(solution)/shard_map/all_to_all | solution.py:461
  79.3 0.0 copy-start.11
  79.3 1.3 %copy-done.11 = bf16[1536,384]{1,0:T(8,128)(2,1)S(1)} copy-done((bf16[1536,384]{1,0:T(8,128)(2,1)S(1)}, bf16[1536,384]{1,0:T(8,128)(2,1)}, u32[]{:S(2)}) %copy-start.11) | copy-done | bytes 1179672
  80.6 1.2 copy-done.13
  81.7 13.8 %shard_map.120 = bf16[1024,384]{1,0:T(8,128)(2,1)} custom-call(s32[2,3]{1,0:T(2,128)S(1)} %copy-done.17, bf16[1024,384]{1,0:T(8,128)(2,1)S(1)} %bitcast.25, bf16[384,1152]{1,0:T(8,128)(2,1)S(1)} %copy-done.13, bf16[384,384]{1,0:T(8,128)(2,1)S(1)} %copy-done.14, bf16[384,1536]{1,0:T(8,128)(2,1)S(1)} %copy-done.9, bf16[1536,384]{1,0:T(8,128)(2,1)S(1)} %copy-done.11), custom_call_target="tpu_custom_call" | custom-call | flops 8999999488 | bytes 4000000 | tf_op jit(solution)/shard_map/pallas_call | solution.py:359
  95.5 4.6 %all-to-all-done.3 = bf16[32,32,384]{2,1,0:T(8,128)(2,1)S(1)} async-done(((bf16[32,32,384]{2,1,0:T(8,128)(2,1)}), bf16[32,32,384]{2,1,0:T(8,128)(2,1)S(1)}, u32[]{:S(2)}, u32[]{:S(2)}) %all-to-all-start.3) | async-done | bytes 786464 | tf_op jit(solution)/shard_map/all_to_all | solution.py:461
  100.1 3.2 %all-to-all-start.1 = ((bf16[32,32,384]{2,1,0:T(8,128)(2,1)}), bf16[32,32,384]{2,1,0:T(8,128)(2,1)S(1)}, u32[]{:S(2)}, u32[]{:S(2)}) async-start(bf16[32,32,384]{2,1,0:T(8,128)(2,1)} %bitcast.8), calls=%async_computation.1 | async-start | bytes 1572864 | tf_op jit(solution)/shard_map/all_to_all | solution.py:461
  103.3 0.0 copy-done
  103.3 1.3 shard_map.124.rest_0_
  104.6 19.6 %all-to-all-done.1 = bf16[32,32,384]{2,1,0:T(8,128)(2,1)S(1)} async-done(((bf16[32,32,384]{2,1,0:T(8,128)(2,1)}), bf16[32,32,384]{2,1,0:T(8,128)(2,1)S(1)}, u32[]{:S(2)}, u32[]{:S(2)}) %all-to-all-start.1) | async-done | bytes 786464 | tf_op jit(solution)/shard_map/all_to_all | solution.py:461
  124.1 1.3 shard_map.125
  (7 shorter events, 0.1 us)
Async XLA Ops:
  1.1 6.5 %collective-permute-start = (bf16[2,16,384]{2,1,0:T(8,128)(2,1)S(1)}, bf16[2,16,384]{2,1,0:T(8,128)(2,1)S(1)}, u32[]{:S(2)}, u32[]{:S(2)}) collective-permute-start(bf16[2,16,384]{2,1,0:T(8,128)(2,1)S(1)} %get-tuple-element.19), channel_id=1, source_target_pairs={{1,2},{2,1},{5,6},{6,5},{9,10},{10,9},{13,14},{14,13},{17,18},{18,... | collective-permute-start | bytes 73736 | tf_op jit(solution)/shard_map/ppermute | solution.py:414
  1.8 6.0 %collective-permute-start.1 = (bf16[2,16,384]{2,1,0:T(8,128)(2,1)S(1)}, bf16[2,16,384]{2,1,0:T(8,128)(2,1)S(1)}, u32[]{:S(2)}, u32[]{:S(2)}) collective-permute-start(bf16[2,16,384]{2,1,0:T(8,128)(2,1)S(1)} %get-tuple-element.20), channel_id=1, source_target_pairs={{0,1},{1,0},{2,3},{3,2},{4,5},{5,4},{6,7},{7,6},{8,9},{9,8},{10,11... | collective-permute-start | bytes 73736 | tf_op jit(solution)/shard_map/ppermute | solution.py:415
  7.9 9.8 %collective-permute-start.3 = (bf16[2,80,384]{2,1,0:T(8,128)(2,1)S(1)}, bf16[2,80,384]{2,1,0:T(8,128)(2,1)S(1)}, u32[]{:S(2)}, u32[]{:S(2)}) collective-permute-start(bf16[2,80,384]{2,1,0:T(8,128)(2,1)S(1)} %get-tuple-element.17), channel_id=1, source_target_pairs={{0,4},{4,0},{8,12},{12,8},{16,20},{20,16},{24,28},{28,24},{1,5},{5... | collective-permute-start | bytes 368648 | tf_op jit(solution)/shard_map/ppermute | solution.py:415
  9.8 7.9 %collective-permute-start.2 = (bf16[2,80,384]{2,1,0:T(8,128)(2,1)S(1)}, bf16[2,80,384]{2,1,0:T(8,128)(2,1)S(1)}, u32[]{:S(2)}, u32[]{:S(2)}) collective-permute-start(bf16[2,80,384]{2,1,0:T(8,128)(2,1)S(1)} %get-tuple-element.18), channel_id=1, source_target_pairs={{4,8},{12,16},{20,24},{8,4},{16,12},{24,20},{5,9},{13,17},{21,25},... | collective-permute-start | bytes 368648 | tf_op jit(solution)/shard_map/ppermute | solution.py:414
  12.8 1.4 %copy-start.1 = (bf16[2,16,64,384]{3,2,1,0:T(8,128)(2,1)S(1)}, bf16[2,16,64,384]{3,2,1,0:T(8,128)(2,1)}, u32[]{:S(2)}) copy-start(bf16[2,16,64,384]{3,2,1,0:T(8,128)(2,1)} %refs_0_.9) | copy-start | bytes 4718596
  14.2 1.3 %copy-start.3 = (bf16[384,1536]{1,0:T(8,128)(2,1)S(1)}, bf16[384,1536]{1,0:T(8,128)(2,1)}, u32[]{:S(2)}) copy-start(bf16[384,1536]{1,0:T(8,128)(2,1)} %refs_4_.6) | copy-start | bytes 3538948
  15.5 2.2 %copy-start.4 = (bf16[384,1536]{1,0:T(8,128)(2,1)S(1)}, bf16[384,1536]{1,0:T(8,128)(2,1)}, u32[]{:S(2)}) copy-start(bf16[384,1536]{1,0:T(8,128)(2,1)} %refs_4_.6) | copy-start | bytes 3538948
  15.5 2.2 %copy-start.7 = (bf16[1536,384]{1,0:T(8,128)(2,1)S(1)}, bf16[1536,384]{1,0:T(8,128)(2,1)}, u32[]{:S(2)}) copy-start(bf16[1536,384]{1,0:T(8,128)(2,1)} %refs_12_.3) | copy-start | bytes 3538948
  15.5 2.2 %copy-start.15 = (f32[3,3,1536]{2,1,0:T(4,128)S(1)}, f32[3,3,1536]{2,1,0:T(4,128)}, u32[]{:S(2)}) copy-start(f32[3,3,1536]{2,1,0:T(4,128)} %refs_5_.6) | copy-start | bytes 165892
  15.5 2.2 %copy-start.16 = (f32[1536]{0:T(1024)S(1)}, f32[1536]{0:T(1024)}, u32[]{:S(2)}) copy-start(f32[1536]{0:T(1024)} %refs_6_.3) | copy-start | bytes 18436
  15.5 2.2 %copy-start.17 = (s32[2,3]{1,0:T(2,128)S(1)}, s32[2,3]{1,0:T(2,128)}, u32[]{:S(2)}) copy-start(s32[2,3]{1,0:T(2,128)} %refs_0_.11) | copy-start | bytes 76
  15.5 2.2 %copy-start.18 = (bf16[128,128]{1,0:T(8,128)(2,1)S(1)}, bf16[128,128]{1,0:T(8,128)(2,1)}, u32[]{:S(2)}) copy-start(bf16[128,128]{1,0:T(8,128)(2,1)} %constant.33.clone.refs_7_) | copy-start | bytes 98308
  27.8 3.6 %copy-start.2 = (bf16[2,16,64,384]{3,2,1,0:T(8,128)(2,1)S(1)}, bf16[2,16,64,384]{3,2,1,0:T(8,128)(2,1)}, u32[]{:S(2)}) copy-start(bf16[2,16,64,384]{3,2,1,0:T(8,128)(2,1)} %refs_0_.9) | copy-start | bytes 4718596
  27.8 24.4 %all-to-all-start.2 = ((bf16[32,32,384]{2,1,0:T(8,128)(2,1)}), bf16[32,32,384]{2,1,0:T(8,128)(2,1)S(1)}, u32[]{:S(2)}, u32[]{:S(2)}) async-start(bf16[32,32,384]{2,1,0:T(8,128)(2,1)} %bitcast.10), calls=%async_computation.2 | async-start | bytes 1572864 | tf_op jit(solution)/shard_map/all_to_all | solution.py:461
  31.3 1.3 %copy-start.5 = (bf16[384,1536]{1,0:T(8,128)(2,1)S(1)}, bf16[384,1536]{1,0:T(8,128)(2,1)}, u32[]{:S(2)}) copy-start(bf16[384,1536]{1,0:T(8,128)(2,1)} %refs_4_.6) | copy-start | bytes 3538948
  32.6 2.1 %copy-start.6 = (bf16[384,1536]{1,0:T(8,128)(2,1)S(1)}, bf16[384,1536]{1,0:T(8,128)(2,1)}, u32[]{:S(2)}) copy-start(bf16[384,1536]{1,0:T(8,128)(2,1)} %refs_4_.6) | copy-start | bytes 3538948
  32.6 2.1 %copy-start.8 = (bf16[1536,384]{1,0:T(8,128)(2,1)S(1)}, bf16[1536,384]{1,0:T(8,128)(2,1)}, u32[]{:S(2)}) copy-start(bf16[1536,384]{1,0:T(8,128)(2,1)} %refs_12_.3) | copy-start | bytes 3538948
  44.7 10.6 %copy-start.9 = (bf16[384,1536]{1,0:T(8,128)(2,1)S(1)}, bf16[384,1536]{1,0:T(8,128)(2,1)}, u32[]{:S(2)}) copy-start(bf16[384,1536]{1,0:T(8,128)(2,1)} %refs_4_.7) | copy-start | bytes 3538948
  44.7 10.6 %copy-start.14 = (bf16[384,384]{1,0:T(8,128)(2,1)S(1)}, bf16[384,384]{1,0:T(8,128)(2,1)}, u32[]{:S(2)}) copy-start(bf16[384,384]{1,0:T(8,128)(2,1)} %refs_3_.3) | copy-start | bytes 884740
  52.2 24.0 %all-to-all-start = ((bf16[32,32,384]{2,1,0:T(8,128)(2,1)}), bf16[32,32,384]{2,1,0:T(8,128)(2,1)S(1)}, u32[]{:S(2)}, u32[]{:S(2)}) async-start(bf16[32,32,384]{2,1,0:T(8,128)(2,1)} %bitcast.6), calls=%async_computation | async-start | bytes 1572864 | tf_op jit(solution)/shard_map/all_to_all | solution.py:461
  55.3 1.3 %copy-start.10 = (bf16[1536,384]{1,0:T(8,128)(2,1)S(1)}, bf16[1536,384]{1,0:T(8,128)(2,1)}, u32[]{:S(2)}) copy-start(bf16[1536,384]{1,0:T(8,128)(2,1)} %refs_5_.7) | copy-start | bytes 3538948
  56.6 1.2 copy-start.12
  76.1 24.0 %all-to-all-start.3 = ((bf16[32,32,384]{2,1,0:T(8,128)(2,1)}), bf16[32,32,384]{2,1,0:T(8,128)(2,1)S(1)}, u32[]{:S(2)}, u32[]{:S(2)}) async-start(bf16[32,32,384]{2,1,0:T(8,128)(2,1)} %bitcast.12), calls=%async_computation.3 | async-start | bytes 1572864 | tf_op jit(solution)/shard_map/all_to_all | solution.py:461
  79.3 1.3 %copy-start.11 = (bf16[1536,384]{1,0:T(8,128)(2,1)S(1)}, bf16[1536,384]{1,0:T(8,128)(2,1)}, u32[]{:S(2)}) copy-start(bf16[1536,384]{1,0:T(8,128)(2,1)} %refs_5_.7) | copy-start | bytes 3538948
  80.6 1.2 copy-start.13
  95.5 7.8 %copy-start = (bf16[128,128]{1,0:T(8,128)(2,1)S(1)}, bf16[128,128]{1,0:T(8,128)(2,1)}, u32[]{:S(2)}) copy-start(bf16[128,128]{1,0:T(8,128)(2,1)} %constant.34.clone.order_ref) | copy-start | bytes 98308
  100.1 24.0 %all-to-all-start.1 = ((bf16[32,32,384]{2,1,0:T(8,128)(2,1)}), bf16[32,32,384]{2,1,0:T(8,128)(2,1)S(1)}, u32[]{:S(2)}, u32[]{:S(2)}) async-start(bf16[32,32,384]{2,1,0:T(8,128)(2,1)} %bitcast.8), calls=%async_computation.1 | async-start | bytes 1572864 | tf_op jit(solution)/shard_map/all_to_all | solution.py:461

commit v2 on v1

--- a/solution.py
+++ b/solution.py
@@ -184,9 +184,13 @@
     place = lax.broadcasted_iota(jnp.int32, (SEG, CHUNK), 0)
     for copy in copies[4:6]:
         copy.wait()
-    for i in range(3):
-        taps[3 * i : 3 * i + 3] = 0.5 * dw_ref[i]
-    taps[9:10] = 0.5 * bias_ref[...].reshape(1, hidden)
+    outside = 0.25 * (dw_ref[0] + dw_ref[2])
+    centre = 0.25 * dw_ref[1]
+    taps[0:3] = 0.5 * dw_ref[0]
+    taps[3:6] = outside + centre
+    taps[6:9] = outside - centre
+    taps[9:12] = 0.5 * dw_ref[2]
+    taps[12:13] = 0.5 * bias_ref[...].reshape(1, hidden)
 
     def expand_halo(c):
         lanes = slice(c * CHUNK, (c + 1) * CHUNK)
@@ -208,25 +212,33 @@
         after = pltpu.roll(plain(r, 0, lanes), SEG - 1, 0)
         edge_cols[r, 1, :, lanes] = jnp.where(place == SEG - 1, side_vals[24 + r : 25 + r, lanes], after)
 
-    def conv_row(c, r):
-        pieces = []
+    def line(r, lanes):
+        if r == 0:
+            middle = edge_rows[0, :, :, lanes]
+        elif r == rows + 1:
+            middle = edge_rows[1, :, :, lanes]
+        else:
+            middle = own_ref[r - 1, :, :, lanes]
+        return jnp.concatenate([edge_cols[r, 0:1, :, lanes], middle, edge_cols[r, 1:2, :, lanes]], axis=0)
+
+    def conv_pair(c, r):
+        upper, lower = [], []
         for lt in range(CHUNK // 128):
             lanes = slice(c * CHUNK + lt * 128, c * CHUNK + (lt + 1) * 128)
-            acc = jnp.broadcast_to(taps[9:10, lanes].reshape(1, 1, 128), (steps, SEG, 128))
-            for i in range(3):
-                if r + i == 0:
-                    middle = edge_rows[0, :, :, lanes]
-                elif r + i == rows + 1:
-                    middle = edge_rows[1, :, :, lanes]
-                else:
-                    middle = own_ref[r + i - 1, :, :, lanes]
-                window = jnp.concatenate(
-                    [edge_cols[r + i, 0:1, :, lanes], middle, edge_cols[r + i, 1:2, :, lanes]], axis=0
-                )
+            d = [line(r + k, lanes) for k in range(4)]
+            mixes = [d[0] - d[2], d[1] + d[2], d[2] - d[1], d[1] - d[3]]
+            products = []
+            for k in range(4):
+                acc = jnp.broadcast_to(taps[12:13, lanes].reshape(1, 1, 128), (steps, SEG, 128)) if k == 1 else None
                 for j in range(3):
-                    acc = acc + window[j : j + steps] * taps[3 * i + j : 3 * i + j + 1, lanes].reshape(1, 1, 128)
-            pieces.append(half_gelu(acc).reshape(cols, 128).astype(BF16))
-        return jnp.concatenate(pieces, axis=1)
+                    term = mixes[k][j : j + steps] * taps[3 * k + j : 3 * k + j + 1, lanes].reshape(1, 1, 128)
+                    acc = term if acc is None else acc + term
+                products.append(acc)
+            first = products[0] + products[1] + products[2]
+            second = products[1] - products[2] - products[3]
+            upper.append(half_gelu(first).reshape(cols, 128).astype(BF16))
+            lower.append(half_gelu(second).reshape(cols, 128).astype(BF16))
+        return jnp.concatenate([jnp.concatenate(upper, axis=1), jnp.concatenate(lower, axis=1)], axis=0)
 
     def project_rows(c, start, stop, values):
         lanes = slice(c * CHUNK, (c + 1) * CHUNK)
@@ -245,8 +257,9 @@
         values, ready = [], None
         for r in range(rows):
             fill_edges(c, r + 2)
-            values.append(conv_row(c, r))
-            if len(values) == part:
+            if r % 2 == 1:
+                values.append(conv_pair(c, r - 1))
+            if 2 * len(values) == part:
                 if ready is not None:
                     project_rows(c, r + 1 - 2 * part, r + 1 - part, ready)
                 ready, values = values, []

time: 126 us -> 125 us (level)
  Pallas kernels: 54.1 us -> 51.8 us
    pallas_call x2, Pallas kernels: 19.9 us -> 17.6 us  [conv_call(): pl.pallas_call(body, in_specs=[pl.BlockSpec(memory_space=pltpu.SMEM)] * 2...]
where the time goes in v2:
time: 125 us; the launch traced here: 124 us
  Pallas kernels  51.8 us (41%)
  waiting for transfers between devices  37.5 us (30%)
  starting transfers between devices  23.3 us (19%)
  local copies, waits for them, and re-layouts  11 us (9%)
    all_to_all x4, waiting for transfers between devices, exchange(): lax.all_to_all(message, ('ha', 'wa'), split_axis=0, concat_axis=0, tiled=...  37.4 us
    pallas_call x2, Pallas kernels, window_call(): pl.pallas_call(body, in_specs=[pl.BlockSpec(memory_space=pltpu.SMEM)] + [...  27.5 us
    pallas_call x2, Pallas kernels, conv_call(): pl.pallas_call(body, in_specs=[pl.BlockSpec(memory_space=pltpu.SMEM)] * 2...  17.6 us
    all_to_all x4, starting transfers between devices, exchange(): lax.all_to_all(message, ('ha', 'wa'), split_axis=0, concat_axis=0, tiled=...  13 us
    unnamed x38, local copies, waits for them, and re-layouts  8.86 us
    ppermute x2, starting transfers between devices, neighbours(): within = lax.ppermute(jnp.where(even, last, first), axis, inner)  6.62 us
    pallas_call x2, Pallas kernels, expand_call(): pl.pallas_call(body, in_specs=[pl.BlockSpec(memory_space=pltpu.VMEM)] * 2...  4.15 us
    ppermute x2, starting transfers between devices, neighbours(): across = lax.ppermute(jnp.where(even, first, last), axis, outer)  3.68 us
  transfers between devices with their start and end apart: 8, of which 5 were waited for; matrix products, arithmetic and copies ran while one was open for 1% of the time, Pallas kernels for 34%

profile of v2, /device:TPU:1, one launch (start us, length us, event | category | flops | bytes accessed | tf_op | source)
XLA Modules:
  0.0 124.2 jit_solution(7000513033741562847)
XLA Ops:
  0.0 1.1 fusion
  1.1 0.7 collective-permute-start
  1.8 4.7 %collective-permute-start.1 = (bf16[2,16,384]{2,1,0:T(8,128)(2,1)S(1)}, bf16[2,16,384]{2,1,0:T(8,128)(2,1)S(1)}, u32[]{:S(2)}, u32[]{:S(2)}) collective-permute-start(bf16[2,16,384]{2,1,0:T(8,128)(2,1)S(1)} %get-tuple-element.20), channel_id=1, source_target_pairs={{0,1},{1,0},{2,3},{3,2},{4,5},{5,4},{6,7},{7,6},{8,9},{9,8},{10,11... | collective-permute-start | bytes 73736 | tf_op jit(solution)/shard_map/ppermute | solution.py:428
  6.5 1.0 slice_bitcast_fusion.1
  7.5 0.1 pad.7.clone
  7.6 0.0 collective-permute-done.refs_10_
  7.6 0.1 collective-permute-done.1.refs_11_
  7.8 0.1 broadcast_select_fusion
  7.9 1.9 %collective-permute-start.3 = (bf16[2,80,384]{2,1,0:T(8,128)(2,1)S(1)}, bf16[2,80,384]{2,1,0:T(8,128)(2,1)S(1)}, u32[]{:S(2)}, u32[]{:S(2)}) collective-permute-start(bf16[2,80,384]{2,1,0:T(8,128)(2,1)S(1)} %get-tuple-element.17), channel_id=1, source_target_pairs={{0,4},{4,0},{8,12},{12,8},{16,20},{20,16},{24,28},{28,24},{1,5},{5... | collective-permute-start | bytes 368648 | tf_op jit(solution)/shard_map/ppermute | solution.py:428
  9.8 3.0 %collective-permute-start.2 = (bf16[2,80,384]{2,1,0:T(8,128)(2,1)S(1)}, bf16[2,80,384]{2,1,0:T(8,128)(2,1)S(1)}, u32[]{:S(2)}, u32[]{:S(2)}) collective-permute-start(bf16[2,80,384]{2,1,0:T(8,128)(2,1)S(1)} %get-tuple-element.18), channel_id=1, source_target_pairs={{4,8},{12,16},{20,24},{8,4},{16,12},{24,20},{5,9},{13,17},{21,25},... | collective-permute-start | bytes 368648 | tf_op jit(solution)/shard_map/ppermute | solution.py:427
  12.8 0.0 copy-start.1
  12.8 1.4 %copy-done.1 = bf16[2,16,64,384]{3,2,1,0:T(8,128)(2,1)S(1)} copy-done((bf16[2,16,64,384]{3,2,1,0:T(8,128)(2,1)S(1)}, bf16[2,16,64,384]{3,2,1,0:T(8,128)(2,1)}, u32[]{:S(2)}) %copy-start.1) | copy-done | bytes 1572888
  14.2 0.0 copy-start.3
  14.2 1.3 %copy-done.3 = bf16[384,1536]{1,0:T(8,128)(2,1)S(1)} copy-done((bf16[384,1536]{1,0:T(8,128)(2,1)S(1)}, bf16[384,1536]{1,0:T(8,128)(2,1)}, u32[]{:S(2)}) %copy-start.3) | copy-done | bytes 1179672
  15.5 0.0 copy-start.4
  15.5 0.0 copy-start.7
  15.5 0.0 copy-start.16
  15.5 0.0 copy-start.17
  15.5 0.0 copy-start.18
  15.6 2.1 %shard_map.121 = (f32[16,8,8,1536]{3,2,1,0:T(8,128)S(1)}, bf16[1024,384]{1,0:T(8,128)(2,1)S(1)}) custom-call(bf16[2,16,64,384]{3,2,1,0:T(8,128)(2,1)S(1)} %copy-done.1, bf16[384,1536]{1,0:T(8,128)(2,1)S(1)} %copy-done.3), custom_call_target="tpu_custom_call" | custom-call | flops 3000000000 | bytes 4000000 | tf_op jit(solution)/shard_map/pallas_call | solution.py:103
  17.6 0.1 add_convert_fusion.refs_1_
  17.7 0.0 collective-permute-done.3.refs_9_
  17.7 0.0 collective-permute-done.2.refs_8_
  17.7 0.0 copy-done.4
  17.7 0.0 copy-done.7
  17.7 0.0 copy-done.15
  17.7 0.0 copy-done.16
  17.8 0.0 copy-done.17
  17.8 0.0 copy-done.18
  17.8 8.8 %shard_map.122 = bf16[1024,384]{1,0:T(8,128)(2,1)} custom-call(s32[2,3]{1,0:T(2,128)S(1)} %copy-done.17, s32[2]{0:T(128)S(1)} %add_convert_fusion.refs_1_, f32[16,8,8,1536]{3,2,1,0:T(8,128)S(1)} %get-tuple-element.11.refs_2_, bf16[1024,384]{1,0:T(8,128)(2,1)S(1)} %get-tuple-element.12.refs_3_, bf16[384,1536]{1,0:T(8,128)(2,1)S(1)} %copy-done.4, ...), custom_call_target="tpu_custom_call" | custom-call | flops 4000000000 | bytes 4000000 | tf_op jit(solution)/shard_map/pallas_call | solution.py:295
  26.6 0.0 copy-start.2
  26.6 3.6 %all-to-all-start.2 = ((bf16[32,32,384]{2,1,0:T(8,128)(2,1)}), bf16[32,32,384]{2,1,0:T(8,128)(2,1)S(1)}, u32[]{:S(2)}, u32[]{:S(2)}) async-start(bf16[32,32,384]{2,1,0:T(8,128)(2,1)} %bitcast.10), calls=%async_computation.2 | async-start | bytes 1572864 | tf_op jit(solution)/shard_map/all_to_all | solution.py:474
  30.2 0.0 copy-done.2
  30.2 0.0 copy-start.5
  30.2 1.3 %copy-done.5 = bf16[384,1536]{1,0:T(8,128)(2,1)S(1)} copy-done((bf16[384,1536]{1,0:T(8,128)(2,1)S(1)}, bf16[384,1536]{1,0:T(8,128)(2,1)}, u32[]{:S(2)}) %copy-start.5) | copy-done | bytes 1179672
  31.5 0.0 copy-start.6
  31.5 0.0 copy-start.8
  31.5 2.1 %shard_map.118 = (f32[16,8,8,1536]{3,2,1,0:T(8,128)S(1)}, bf16[1024,384]{1,0:T(8,128)(2,1)S(1)}) custom-call(bf16[2,16,64,384]{3,2,1,0:T(8,128)(2,1)S(1)} %copy-done.2, bf16[384,1536]{1,0:T(8,128)(2,1)S(1)} %copy-done.5), custom_call_target="tpu_custom_call" | custom-call | flops 3000000000 | bytes 4000000 | tf_op jit(solution)/shard_map/pallas_call | solution.py:103
  33.5 0.0 copy-done.6
  33.6 0.0 copy-done.8
  33.6 8.8 %shard_map.119 = bf16[1024,384]{1,0:T(8,128)(2,1)} custom-call(s32[2,3]{1,0:T(2,128)S(1)} %copy-done.17, s32[2]{0:T(128)S(1)} %add_convert_fusion.refs_1_, f32[16,8,8,1536]{3,2,1,0:T(8,128)S(1)} %get-tuple-element.9.refs_2_, bf16[1024,384]{1,0:T(8,128)(2,1)S(1)} %get-tuple-element.10.refs_3_, bf16[384,1536]{1,0:T(8,128)(2,1)S(1)} %copy-done.6, ...), custom_call_target="tpu_custom_call" | custom-call | flops 4000000000 | bytes 4000000 | tf_op jit(solution)/shard_map/pallas_call | solution.py:295
  42.4 0.0 copy-start.9
  42.4 0.0 copy-start.14
  42.4 8.6 %all-to-all-done.2 = bf16[32,32,384]{2,1,0:T(8,128)(2,1)S(1)} async-done(((bf16[32,32,384]{2,1,0:T(8,128)(2,1)}), bf16[32,32,384]{2,1,0:T(8,128)(2,1)S(1)}, u32[]{:S(2)}, u32[]{:S(2)}) %all-to-all-start.2) | async-done | bytes 786464 | tf_op jit(solution)/shard_map/all_to_all | solution.py:474
  51.0 3.2 %all-to-all-start = ((bf16[32,32,384]{2,1,0:T(8,128)(2,1)}), bf16[32,32,384]{2,1,0:T(8,128)(2,1)S(1)}, u32[]{:S(2)}, u32[]{:S(2)}) async-start(bf16[32,32,384]{2,1,0:T(8,128)(2,1)} %bitcast.6), calls=%async_computation | async-start | bytes 1572864 | tf_op jit(solution)/shard_map/all_to_all | solution.py:474
  54.2 0.0 copy-done.9
  54.2 0.0 copy-done.14
  54.2 0.0 copy-start.10
  54.2 1.3 %copy-done.10 = bf16[1536,384]{1,0:T(8,128)(2,1)S(1)} copy-done((bf16[1536,384]{1,0:T(8,128)(2,1)S(1)}, bf16[1536,384]{1,0:T(8,128)(2,1)}, u32[]{:S(2)}) %copy-start.10) | copy-done | bytes 1179672
  55.4 0.0 copy-start.12
  55.4 1.2 copy-done.12
  56.6 13.8 %shard_map.123 = bf16[1024,384]{1,0:T(8,128)(2,1)} custom-call(s32[2,3]{1,0:T(2,128)S(1)} %copy-done.17, bf16[1024,384]{1,0:T(8,128)(2,1)S(1)} %bitcast.24, bf16[384,1152]{1,0:T(8,128)(2,1)S(1)} %copy-done.12, bf16[384,384]{1,0:T(8,128)(2,1)S(1)} %copy-done.14, bf16[384,1536]{1,0:T(8,128)(2,1)S(1)} %copy-done.9, bf16[1536,384]{1,0:T(8,128)(2,1)S(1)} %copy-done.10), custom_call_target="tpu_custom_call" | custom-call | flops 8999999488 | bytes 4000000 | tf_op jit(solution)/shard_map/pallas_call | solution.py:372
  70.4 4.6 %all-to-all-done = bf16[32,32,384]{2,1,0:T(8,128)(2,1)S(1)} async-done(((bf16[32,32,384]{2,1,0:T(8,128)(2,1)}), bf16[32,32,384]{2,1,0:T(8,128)(2,1)S(1)}, u32[]{:S(2)}, u32[]{:S(2)}) %all-to-all-start) | async-done | bytes 786464 | tf_op jit(solution)/shard_map/all_to_all | solution.py:474
  75.0 3.2 %all-to-all-start.3 = ((bf16[32,32,384]{2,1,0:T(8,128)(2,1)}), bf16[32,32,384]{2,1,0:T(8,128)(2,1)S(1)}, u32[]{:S(2)}, u32[]{:S(2)}) async-start(bf16[32,32,384]{2,1,0:T(8,128)(2,1)} %bitcast.12), calls=%async_computation.3 | async-start | bytes 1572864 | tf_op jit(solution)/shard_map/all_to_all | solution.py:474
  78.1 0.0 copy-start.11
  78.2 1.3 %copy-done.11 = bf16[1536,384]{1,0:T(8,128)(2,1)S(1)} copy-done((bf16[1536,384]{1,0:T(8,128)(2,1)S(1)}, bf16[1536,384]{1,0:T(8,128)(2,1)}, u32[]{:S(2)}) %copy-start.11) | copy-done | bytes 1179672
  79.4 1.2 copy-done.13
  80.6 13.8 %shard_map.120 = bf16[1024,384]{1,0:T(8,128)(2,1)} custom-call(s32[2,3]{1,0:T(2,128)S(1)} %copy-done.17, bf16[1024,384]{1,0:T(8,128)(2,1)S(1)} %bitcast.25, bf16[384,1152]{1,0:T(8,128)(2,1)S(1)} %copy-done.13, bf16[384,384]{1,0:T(8,128)(2,1)S(1)} %copy-done.14, bf16[384,1536]{1,0:T(8,128)(2,1)S(1)} %copy-done.9, bf16[1536,384]{1,0:T(8,128)(2,1)S(1)} %copy-done.11), custom_call_target="tpu_custom_call" | custom-call | flops 8999999488 | bytes 4000000 | tf_op jit(solution)/shard_map/pallas_call | solution.py:372
  94.4 4.6 %all-to-all-done.3 = bf16[32,32,384]{2,1,0:T(8,128)(2,1)S(1)} async-done(((bf16[32,32,384]{2,1,0:T(8,128)(2,1)}), bf16[32,32,384]{2,1,0:T(8,128)(2,1)S(1)}, u32[]{:S(2)}, u32[]{:S(2)}) %all-to-all-start.3) | async-done | bytes 786464 | tf_op jit(solution)/shard_map/all_to_all | solution.py:474
  99.0 3.2 %all-to-all-start.1 = ((bf16[32,32,384]{2,1,0:T(8,128)(2,1)}), bf16[32,32,384]{2,1,0:T(8,128)(2,1)S(1)}, u32[]{:S(2)}, u32[]{:S(2)}) async-start(bf16[32,32,384]{2,1,0:T(8,128)(2,1)} %bitcast.8), calls=%async_computation.1 | async-start | bytes 1572864 | tf_op jit(solution)/shard_map/all_to_all | solution.py:474
  102.1 0.0 copy-done
  102.1 1.2 %shard_map.124.rest_0_ = bf16[2,16,64,384]{3,2,1,0:T(8,128)(2,1)} custom-call(bf16[1024,384]{1,0:T(8,128)(2,1)S(1)} %bitcast.22, bf16[128,128]{1,0:T(8,128)(2,1)S(1)} %copy-done), custom_call_target="tpu_custom_call" | custom-call | flops 100000000 | bytes 2000000 | tf_op jit(solution)/shard_map/pallas_call | solution.py:409
  103.4 19.6 %all-to-all-done.1 = bf16[32,32,384]{2,1,0:T(8,128)(2,1)S(1)} async-done(((bf16[32,32,384]{2,1,0:T(8,128)(2,1)}), bf16[32,32,384]{2,1,0:T(8,128)(2,1)S(1)}, u32[]{:S(2)}, u32[]{:S(2)}) %all-to-all-start.1) | async-done | bytes 786464 | tf_op jit(solution)/shard_map/all_to_all | solution.py:474
  123.0 1.3 %shard_map.125 = bf16[2,16,64,384]{3,2,1,0:T(8,128)(2,1)} custom-call(bf16[1024,384]{1,0:T(8,128)(2,1)S(1)} %bitcast.23, bf16[128,128]{1,0:T(8,128)(2,1)S(1)} %copy-done, bf16[2,16,64,384]{3,2,1,0:T(8,128)(2,1)} %shard_map.124.rest_0_), custom_call_target="tpu_custom_call", output_to_operand_aliasing={{}: (2, {})} | custom-call | flops 100000000 | bytes 2000000 | tf_op jit(solution)/shard_map/pallas_call | solution.py:409
  (7 shorter events, 0.1 us)
Async XLA Ops:
  1.1 6.5 %collective-permute-start = (bf16[2,16,384]{2,1,0:T(8,128)(2,1)S(1)}, bf16[2,16,384]{2,1,0:T(8,128)(2,1)S(1)}, u32[]{:S(2)}, u32[]{:S(2)}) collective-permute-start(bf16[2,16,384]{2,1,0:T(8,128)(2,1)S(1)} %get-tuple-element.19), channel_id=1, source_target_pairs={{1,2},{2,1},{5,6},{6,5},{9,10},{10,9},{13,14},{14,13},{17,18},{18,... | collective-permute-start | bytes 73736 | tf_op jit(solution)/shard_map/ppermute | solution.py:427
  1.8 6.0 %collective-permute-start.1 = (bf16[2,16,384]{2,1,0:T(8,128)(2,1)S(1)}, bf16[2,16,384]{2,1,0:T(8,128)(2,1)S(1)}, u32[]{:S(2)}, u32[]{:S(2)}) collective-permute-start(bf16[2,16,384]{2,1,0:T(8,128)(2,1)S(1)} %get-tuple-element.20), channel_id=1, source_target_pairs={{0,1},{1,0},{2,3},{3,2},{4,5},{5,4},{6,7},{7,6},{8,9},{9,8},{10,11... | collective-permute-start | bytes 73736 | tf_op jit(solution)/shard_map/ppermute | solution.py:428
  7.9 9.8 %collective-permute-start.3 = (bf16[2,80,384]{2,1,0:T(8,128)(2,1)S(1)}, bf16[2,80,384]{2,1,0:T(8,128)(2,1)S(1)}, u32[]{:S(2)}, u32[]{:S(2)}) collective-permute-start(bf16[2,80,384]{2,1,0:T(8,128)(2,1)S(1)} %get-tuple-element.17), channel_id=1, source_target_pairs={{0,4},{4,0},{8,12},{12,8},{16,20},{20,16},{24,28},{28,24},{1,5},{5... | collective-permute-start | bytes 368648 | tf_op jit(solution)/shard_map/ppermute | solution.py:428
  9.8 7.9 %collective-permute-start.2 = (bf16[2,80,384]{2,1,0:T(8,128)(2,1)S(1)}, bf16[2,80,384]{2,1,0:T(8,128)(2,1)S(1)}, u32[]{:S(2)}, u32[]{:S(2)}) collective-permute-start(bf16[2,80,384]{2,1,0:T(8,128)(2,1)S(1)} %get-tuple-element.18), channel_id=1, source_target_pairs={{4,8},{12,16},{20,24},{8,4},{16,12},{24,20},{5,9},{13,17},{21,25},... | collective-permute-start | bytes 368648 | tf_op jit(solution)/shard_map/ppermute | solution.py:427
  12.8 1.4 %copy-start.1 = (bf16[2,16,64,384]{3,2,1,0:T(8,128)(2,1)S(1)}, bf16[2,16,64,384]{3,2,1,0:T(8,128)(2,1)}, u32[]{:S(2)}) copy-start(bf16[2,16,64,384]{3,2,1,0:T(8,128)(2,1)} %refs_0_.9) | copy-start | bytes 4718596
  14.2 1.3 %copy-start.3 = (bf16[384,1536]{1,0:T(8,128)(2,1)S(1)}, bf16[384,1536]{1,0:T(8,128)(2,1)}, u32[]{:S(2)}) copy-start(bf16[384,1536]{1,0:T(8,128)(2,1)} %refs_4_.6) | copy-start | bytes 3538948
  15.5 2.2 %copy-start.4 = (bf16[384,1536]{1,0:T(8,128)(2,1)S(1)}, bf16[384,1536]{1,0:T(8,128)(2,1)}, u32[]{:S(2)}) copy-start(bf16[384,1536]{1,0:T(8,128)(2,1)} %refs_4_.6) | copy-start | bytes 3538948
  15.5 2.2 %copy-start.7 = (bf16[1536,384]{1,0:T(8,128)(2,1)S(1)}, bf16[1536,384]{1,0:T(8,128)(2,1)}, u32[]{:S(2)}) copy-start(bf16[1536,384]{1,0:T(8,128)(2,1)} %refs_12_.3) | copy-start | bytes 3538948
  15.5 2.2 %copy-start.15 = (f32[3,3,1536]{2,1,0:T(4,128)S(1)}, f32[3,3,1536]{2,1,0:T(4,128)}, u32[]{:S(2)}) copy-start(f32[3,3,1536]{2,1,0:T(4,128)} %refs_5_.6) | copy-start | bytes 165892
  15.5 2.2 %copy-start.16 = (f32[1536]{0:T(1024)S(1)}, f32[1536]{0:T(1024)}, u32[]{:S(2)}) copy-start(f32[1536]{0:T(1024)} %refs_6_.3) | copy-start | bytes 18436
  15.5 2.2 %copy-start.17 = (s32[2,3]{1,0:T(2,128)S(1)}, s32[2,3]{1,0:T(2,128)}, u32[]{:S(2)}) copy-start(s32[2,3]{1,0:T(2,128)} %refs_0_.11) | copy-start | bytes 76
  15.5 2.2 %copy-start.18 = (bf16[128,128]{1,0:T(8,128)(2,1)S(1)}, bf16[128,128]{1,0:T(8,128)(2,1)}, u32[]{:S(2)}) copy-start(bf16[128,128]{1,0:T(8,128)(2,1)} %constant.33.clone.refs_7_) | copy-start | bytes 98308
  26.6 3.6 %copy-start.2 = (bf16[2,16,64,384]{3,2,1,0:T(8,128)(2,1)S(1)}, bf16[2,16,64,384]{3,2,1,0:T(8,128)(2,1)}, u32[]{:S(2)}) copy-start(bf16[2,16,64,384]{3,2,1,0:T(8,128)(2,1)} %refs_0_.9) | copy-start | bytes 4718596
  26.6 24.4 %all-to-all-start.2 = ((bf16[32,32,384]{2,1,0:T(8,128)(2,1)}), bf16[32,32,384]{2,1,0:T(8,128)(2,1)S(1)}, u32[]{:S(2)}, u32[]{:S(2)}) async-start(bf16[32,32,384]{2,1,0:T(8,128)(2,1)} %bitcast.10), calls=%async_computation.2 | async-start | bytes 1572864 | tf_op jit(solution)/shard_map/all_to_all | solution.py:474
  30.2 1.3 %copy-start.5 = (bf16[384,1536]{1,0:T(8,128)(2,1)S(1)}, bf16[384,1536]{1,0:T(8,128)(2,1)}, u32[]{:S(2)}) copy-start(bf16[384,1536]{1,0:T(8,128)(2,1)} %refs_4_.6) | copy-start | bytes 3538948
  31.5 2.1 %copy-start.6 = (bf16[384,1536]{1,0:T(8,128)(2,1)S(1)}, bf16[384,1536]{1,0:T(8,128)(2,1)}, u32[]{:S(2)}) copy-start(bf16[384,1536]{1,0:T(8,128)(2,1)} %refs_4_.6) | copy-start | bytes 3538948
  31.5 2.1 %copy-start.8 = (bf16[1536,384]{1,0:T(8,128)(2,1)S(1)}, bf16[1536,384]{1,0:T(8,128)(2,1)}, u32[]{:S(2)}) copy-start(bf16[1536,384]{1,0:T(8,128)(2,1)} %refs_12_.3) | copy-start | bytes 3538948
  42.4 11.8 %copy-start.9 = (bf16[384,1536]{1,0:T(8,128)(2,1)S(1)}, bf16[384,1536]{1,0:T(8,128)(2,1)}, u32[]{:S(2)}) copy-start(bf16[384,1536]{1,0:T(8,128)(2,1)} %refs_4_.7) | copy-start | bytes 3538948
  42.4 11.8 %copy-start.14 = (bf16[384,384]{1,0:T(8,128)(2,1)S(1)}, bf16[384,384]{1,0:T(8,128)(2,1)}, u32[]{:S(2)}) copy-start(bf16[384,384]{1,0:T(8,128)(2,1)} %refs_3_.3) | copy-start | bytes 884740
  51.0 24.0 %all-to-all-start = ((bf16[32,32,384]{2,1,0:T(8,128)(2,1)}), bf16[32,32,384]{2,1,0:T(8,128)(2,1)S(1)}, u32[]{:S(2)}, u32[]{:S(2)}) async-start(bf16[32,32,384]{2,1,0:T(8,128)(2,1)} %bitcast.6), calls=%async_computation | async-start | bytes 1572864 | tf_op jit(solution)/shard_map/all_to_all | solution.py:474
  54.2 1.3 %copy-start.10 = (bf16[1536,384]{1,0:T(8,128)(2,1)S(1)}, bf16[1536,384]{1,0:T(8,128)(2,1)}, u32[]{:S(2)}) copy-start(bf16[1536,384]{1,0:T(8,128)(2,1)} %refs_5_.7) | copy-start | bytes 3538948
  55.4 1.2 copy-start.12
  75.0 24.0 %all-to-all-start.3 = ((bf16[32,32,384]{2,1,0:T(8,128)(2,1)}), bf16[32,32,384]{2,1,0:T(8,128)(2,1)S(1)}, u32[]{:S(2)}, u32[]{:S(2)}) async-start(bf16[32,32,384]{2,1,0:T(8,128)(2,1)} %bitcast.12), calls=%async_computation.3 | async-start | bytes 1572864 | tf_op jit(solution)/shard_map/all_to_all | solution.py:474
  78.1 1.3 %copy-start.11 = (bf16[1536,384]{1,0:T(8,128)(2,1)S(1)}, bf16[1536,384]{1,0:T(8,128)(2,1)}, u32[]{:S(2)}) copy-start(bf16[1536,384]{1,0:T(8,128)(2,1)} %refs_5_.7) | copy-start | bytes 3538948
  79.4 1.2 copy-start.13
  94.4 7.8 %copy-start = (bf16[128,128]{1,0:T(8,128)(2,1)S(1)}, bf16[128,128]{1,0:T(8,128)(2,1)}, u32[]{:S(2)}) copy-start(bf16[128,128]{1,0:T(8,128)(2,1)} %constant.34.clone.order_ref) | copy-start | bytes 98308
  99.0 24.0 %all-to-all-start.1 = ((bf16[32,32,384]{2,1,0:T(8,128)(2,1)}), bf16[32,32,384]{2,1,0:T(8,128)(2,1)S(1)}, u32[]{:S(2)}, u32[]{:S(2)}) async-start(bf16[32,32,384]{2,1,0:T(8,128)(2,1)} %bitcast.8), calls=%async_computation.1 | async-start | bytes 1572864 | tf_op jit(solution)/shard_map/all_to_all | solution.py:474

commit v3 on v2

--- a/solution.py
+++ b/solution.py
@@ -380,38 +380,44 @@
     )(keep, x, qkv_weight, out_weight, mlp_in, mlp_out)
 
 
-def restore_kernel(x_ref, order_ref, *rest):
-    out_ref = rest[-1]
-    _, rows, cols, channels = out_ref.shape
+def restore_kernel(frame, x_ref, order_ref, *rest):
+    out_any, rows_ref, sems = rest[-3:]
+    rows, cols, channels = rows_ref.shape
     span = order_ref.shape[0]
     groups = span // cols
     stride = rows // groups
     order = order_ref[...]
+    copies = []
     for d in range(stride):
         back = dot(order, x_ref[d * span : (d + 1) * span]).astype(BF16)
         for g in range(groups):
-            out_ref[0, g * stride + d] = back[g * cols : (g + 1) * cols]
+            r = g * stride + d
+            rows_ref[r] = back[g * cols : (g + 1) * cols]
+            copies.append(pltpu.make_async_copy(rows_ref.at[r], out_any.at[frame, r], sems.at[r]))
+            copies[-1].start()
+    for copy in copies:
+        copy.wait()
 
 
 def restore_call(frame, x, order, out_shape, previous):
     _, rows, cols, channels = out_shape
 
-    def whole(a):
-        return pl.BlockSpec(a.shape, lambda i, n=a.ndim: (0,) * n)
+    def body(*refs):
+        restore_kernel(frame, *refs)
 
     args = [x, order]
-    specs = [whole(a) for a in args]
+    specs = [pl.BlockSpec(memory_space=pltpu.VMEM)] * 2
     aliases = {}
     if previous is not None:
         aliases = {len(args): 0}
         args.append(previous)
         specs.append(pl.BlockSpec(memory_space=pl.ANY))
     return pl.pallas_call(
-        restore_kernel,
-        grid=(1,),
+        body,
         in_specs=specs,
-        out_specs=pl.BlockSpec((1, rows, cols, channels), lambda i: (frame, 0, 0, 0)),
+        out_specs=pl.BlockSpec(memory_space=pl.ANY),
         out_shape=jax.ShapeDtypeStruct(out_shape, BF16),
+        scratch_shapes=[pltpu.VMEM((rows, cols, channels), BF16), pltpu.SemaphoreType.DMA((rows,))],
         input_output_aliases=aliases,
         compiler_params=pltpu.CompilerParams(vmem_limit_bytes=16 * MIB),
         cost_estimate=pl.CostEstimate(flops=10**8, bytes_accessed=2 * 10**6, transcendentals=0),

time: 125 us -> 125 us (level)
  no operation moved by 1% of the time
where the time goes in v3:
time: 125 us; the launch traced here: 124 us
  Pallas kernels  51.7 us (41%)
  waiting for transfers between devices  37.6 us (30%)
  starting transfers between devices  23.3 us (19%)
  local copies, waits for them, and re-layouts  11 us (9%)
    all_to_all x4, waiting for transfers between devices, exchange(): lax.all_to_all(message, ('ha', 'wa'), split_axis=0, concat_axis=0, tiled=...  37.4 us
    pallas_call x2, Pallas kernels, window_call(): pl.pallas_call(body, in_specs=[pl.BlockSpec(memory_space=pltpu.SMEM)] + [...  27.5 us
    pallas_call x2, Pallas kernels, conv_call(): pl.pallas_call(body, in_specs=[pl.BlockSpec(memory_space=pltpu.SMEM)] * 2...  17.6 us
    all_to_all x4, starting transfers between devices, exchange(): lax.all_to_all(message, ('ha', 'wa'), split_axis=0, concat_axis=0, tiled=...  13 us
    unnamed x38, local copies, waits for them, and re-layouts  8.86 us
    ppermute x2, starting transfers between devices, neighbours(): within = lax.ppermute(jnp.where(even, last, first), axis, inner)  6.62 us
    pallas_call x2, Pallas kernels, expand_call(): pl.pallas_call(body, in_specs=[pl.BlockSpec(memory_space=pltpu.VMEM)] * 2...  4.15 us
    ppermute x2, starting transfers between devices, neighbours(): across = lax.ppermute(jnp.where(even, first, last), axis, outer)  3.68 us
  transfers between devices with their start and end apart: 8, of which 5 were waited for; matrix products, arithmetic and copies ran while one was open for 1% of the time, Pallas kernels for 34%

profile of v3, /device:TPU:1, one launch (start us, length us, event | category | flops | bytes accessed | tf_op | source)
XLA Modules:
  0.0 124.3 jit_solution(1071418755187821050)
XLA Ops:
  0.0 1.1 fusion
  1.1 0.7 collective-permute-start
  1.8 4.7 %collective-permute-start.1 = (bf16[2,16,384]{2,1,0:T(8,128)(2,1)S(1)}, bf16[2,16,384]{2,1,0:T(8,128)(2,1)S(1)}, u32[]{:S(2)}, u32[]{:S(2)}) collective-permute-start(bf16[2,16,384]{2,1,0:T(8,128)(2,1)S(1)} %get-tuple-element.20), channel_id=1, source_target_pairs={{0,1},{1,0},{2,3},{3,2},{4,5},{5,4},{6,7},{7,6},{8,9},{9,8},{10,11... | collective-permute-start | bytes 73736 | tf_op jit(solution)/shard_map/ppermute | solution.py:434
  6.5 1.0 slice_bitcast_fusion.1
  7.5 0.1 pad.7.clone
  7.6 0.0 collective-permute-done.refs_10_
  7.6 0.1 collective-permute-done.1.refs_11_
  7.8 0.1 broadcast_select_fusion
  7.9 1.9 %collective-permute-start.3 = (bf16[2,80,384]{2,1,0:T(8,128)(2,1)S(1)}, bf16[2,80,384]{2,1,0:T(8,128)(2,1)S(1)}, u32[]{:S(2)}, u32[]{:S(2)}) collective-permute-start(bf16[2,80,384]{2,1,0:T(8,128)(2,1)S(1)} %get-tuple-element.17), channel_id=1, source_target_pairs={{0,4},{4,0},{8,12},{12,8},{16,20},{20,16},{24,28},{28,24},{1,5},{5... | collective-permute-start | bytes 368648 | tf_op jit(solution)/shard_map/ppermute | solution.py:434
  9.8 3.0 %collective-permute-start.2 = (bf16[2,80,384]{2,1,0:T(8,128)(2,1)S(1)}, bf16[2,80,384]{2,1,0:T(8,128)(2,1)S(1)}, u32[]{:S(2)}, u32[]{:S(2)}) collective-permute-start(bf16[2,80,384]{2,1,0:T(8,128)(2,1)S(1)} %get-tuple-element.18), channel_id=1, source_target_pairs={{4,8},{12,16},{20,24},{8,4},{16,12},{24,20},{5,9},{13,17},{21,25},... | collective-permute-start | bytes 368648 | tf_op jit(solution)/shard_map/ppermute | solution.py:433
  12.8 0.0 copy-start.1
  12.8 1.4 %copy-done.1 = bf16[2,16,64,384]{3,2,1,0:T(8,128)(2,1)S(1)} copy-done((bf16[2,16,64,384]{3,2,1,0:T(8,128)(2,1)S(1)}, bf16[2,16,64,384]{3,2,1,0:T(8,128)(2,1)}, u32[]{:S(2)}) %copy-start.1) | copy-done | bytes 1572888
  14.2 0.0 copy-start.3
  14.2 1.3 %copy-done.3 = bf16[384,1536]{1,0:T(8,128)(2,1)S(1)} copy-done((bf16[384,1536]{1,0:T(8,128)(2,1)S(1)}, bf16[384,1536]{1,0:T(8,128)(2,1)}, u32[]{:S(2)}) %copy-start.3) | copy-done | bytes 1179672
  15.5 0.0 copy-start.4
  15.5 0.0 copy-start.7
  15.5 0.0 copy-start.15
  15.5 0.0 copy-start.16
  15.5 0.0 copy-start.17
  15.5 0.0 copy-start.18
  15.6 2.1 %shard_map.121 = (f32[16,8,8,1536]{3,2,1,0:T(8,128)S(1)}, bf16[1024,384]{1,0:T(8,128)(2,1)S(1)}) custom-call(bf16[2,16,64,384]{3,2,1,0:T(8,128)(2,1)S(1)} %copy-done.1, bf16[384,1536]{1,0:T(8,128)(2,1)S(1)} %copy-done.3), custom_call_target="tpu_custom_call" | custom-call | flops 3000000000 | bytes 4000000 | tf_op jit(solution)/shard_map/pallas_call | solution.py:103
  17.6 0.1 add_convert_fusion.refs_1_
  17.7 0.0 collective-permute-done.3.refs_9_
  17.7 0.0 collective-permute-done.2.refs_8_
  17.7 0.0 copy-done.4
  17.7 0.0 copy-done.7
  17.7 0.0 copy-done.15
  17.7 0.0 copy-done.16
  17.8 0.0 copy-done.17
  17.8 0.0 copy-done.18
  17.8 8.8 %shard_map.122 = bf16[1024,384]{1,0:T(8,128)(2,1)} custom-call(s32[2,3]{1,0:T(2,128)S(1)} %copy-done.17, s32[2]{0:T(128)S(1)} %add_convert_fusion.refs_1_, f32[16,8,8,1536]{3,2,1,0:T(8,128)S(1)} %get-tuple-element.11.refs_2_, bf16[1024,384]{1,0:T(8,128)(2,1)S(1)} %get-tuple-element.12.refs_3_, bf16[384,1536]{1,0:T(8,128)(2,1)S(1)} %copy-done.4, ...), custom_call_target="tpu_custom_call" | custom-call | flops 4000000000 | bytes 4000000 | tf_op jit(solution)/shard_map/pallas_call | solution.py:295
  26.6 0.0 copy-start.2
  26.6 3.6 %all-to-all-start.2 = ((bf16[32,32,384]{2,1,0:T(8,128)(2,1)}), bf16[32,32,384]{2,1,0:T(8,128)(2,1)S(1)}, u32[]{:S(2)}, u32[]{:S(2)}) async-start(bf16[32,32,384]{2,1,0:T(8,128)(2,1)} %bitcast.10), calls=%async_computation.2 | async-start | bytes 1572864 | tf_op jit(solution)/shard_map/all_to_all | solution.py:480
  30.2 0.0 copy-done.2
  30.2 0.0 copy-start.5
  30.2 1.3 %copy-done.5 = bf16[384,1536]{1,0:T(8,128)(2,1)S(1)} copy-done((bf16[384,1536]{1,0:T(8,128)(2,1)S(1)}, bf16[384,1536]{1,0:T(8,128)(2,1)}, u32[]{:S(2)}) %copy-start.5) | copy-done | bytes 1179672
  31.5 0.0 copy-start.8
  31.5 2.1 %shard_map.118 = (f32[16,8,8,1536]{3,2,1,0:T(8,128)S(1)}, bf16[1024,384]{1,0:T(8,128)(2,1)S(1)}) custom-call(bf16[2,16,64,384]{3,2,1,0:T(8,128)(2,1)S(1)} %copy-done.2, bf16[384,1536]{1,0:T(8,128)(2,1)S(1)} %copy-done.5), custom_call_target="tpu_custom_call" | custom-call | flops 3000000000 | bytes 4000000 | tf_op jit(solution)/shard_map/pallas_call | solution.py:103
  33.5 0.0 copy-done.6
  33.6 0.0 copy-done.8
  33.6 8.8 %shard_map.119 = bf16[1024,384]{1,0:T(8,128)(2,1)} custom-call(s32[2,3]{1,0:T(2,128)S(1)} %copy-done.17, s32[2]{0:T(128)S(1)} %add_convert_fusion.refs_1_, f32[16,8,8,1536]{3,2,1,0:T(8,128)S(1)} %get-tuple-element.9.refs_2_, bf16[1024,384]{1,0:T(8,128)(2,1)S(1)} %get-tuple-element.10.refs_3_, bf16[384,1536]{1,0:T(8,128)(2,1)S(1)} %copy-done.6, ...), custom_call_target="tpu_custom_call" | custom-call | flops 4000000000 | bytes 4000000 | tf_op jit(solution)/shard_map/pallas_call | solution.py:295
  42.4 0.0 copy-start.9
  42.4 0.0 copy-start.14
  42.4 8.6 %all-to-all-done.2 = bf16[32,32,384]{2,1,0:T(8,128)(2,1)S(1)} async-done(((bf16[32,32,384]{2,1,0:T(8,128)(2,1)}), bf16[32,32,384]{2,1,0:T(8,128)(2,1)S(1)}, u32[]{:S(2)}, u32[]{:S(2)}) %all-to-all-start.2) | async-done | bytes 786464 | tf_op jit(solution)/shard_map/all_to_all | solution.py:480
  51.0 3.2 %all-to-all-start = ((bf16[32,32,384]{2,1,0:T(8,128)(2,1)}), bf16[32,32,384]{2,1,0:T(8,128)(2,1)S(1)}, u32[]{:S(2)}, u32[]{:S(2)}) async-start(bf16[32,32,384]{2,1,0:T(8,128)(2,1)} %bitcast.6), calls=%async_computation | async-start | bytes 1572864 | tf_op jit(solution)/shard_map/all_to_all | solution.py:480
  54.2 0.0 copy-done.9
  54.2 0.0 copy-done.14
  54.2 0.0 copy-start.10
  54.2 1.3 %copy-done.10 = bf16[1536,384]{1,0:T(8,128)(2,1)S(1)} copy-done((bf16[1536,384]{1,0:T(8,128)(2,1)S(1)}, bf16[1536,384]{1,0:T(8,128)(2,1)}, u32[]{:S(2)}) %copy-start.10) | copy-done | bytes 1179672
  55.4 0.0 copy-start.12
  55.4 1.2 copy-done.12
  56.6 13.8 %shard_map.123 = bf16[1024,384]{1,0:T(8,128)(2,1)} custom-call(s32[2,3]{1,0:T(2,128)S(1)} %copy-done.17, bf16[1024,384]{1,0:T(8,128)(2,1)S(1)} %bitcast.24, bf16[384,1152]{1,0:T(8,128)(2,1)S(1)} %copy-done.12, bf16[384,384]{1,0:T(8,128)(2,1)S(1)} %copy-done.14, bf16[384,1536]{1,0:T(8,128)(2,1)S(1)} %copy-done.9, bf16[1536,384]{1,0:T(8,128)(2,1)S(1)} %copy-done.10), custom_call_target="tpu_custom_call" | custom-call | flops 8999999488 | bytes 4000000 | tf_op jit(solution)/shard_map/pallas_call | solution.py:372
  70.4 4.6 %all-to-all-done = bf16[32,32,384]{2,1,0:T(8,128)(2,1)S(1)} async-done(((bf16[32,32,384]{2,1,0:T(8,128)(2,1)}), bf16[32,32,384]{2,1,0:T(8,128)(2,1)S(1)}, u32[]{:S(2)}, u32[]{:S(2)}) %all-to-all-start) | async-done | bytes 786464 | tf_op jit(solution)/shard_map/all_to_all | solution.py:480
  75.0 3.2 %all-to-all-start.3 = ((bf16[32,32,384]{2,1,0:T(8,128)(2,1)}), bf16[32,32,384]{2,1,0:T(8,128)(2,1)S(1)}, u32[]{:S(2)}, u32[]{:S(2)}) async-start(bf16[32,32,384]{2,1,0:T(8,128)(2,1)} %bitcast.12), calls=%async_computation.3 | async-start | bytes 1572864 | tf_op jit(solution)/shard_map/all_to_all | solution.py:480
  78.1 0.0 copy-start.11
  78.2 1.3 %copy-done.11 = bf16[1536,384]{1,0:T(8,128)(2,1)S(1)} copy-done((bf16[1536,384]{1,0:T(8,128)(2,1)S(1)}, bf16[1536,384]{1,0:T(8,128)(2,1)}, u32[]{:S(2)}) %copy-start.11) | copy-done | bytes 1179672
  79.4 1.2 copy-done.13
  80.6 13.8 %shard_map.120 = bf16[1024,384]{1,0:T(8,128)(2,1)} custom-call(s32[2,3]{1,0:T(2,128)S(1)} %copy-done.17, bf16[1024,384]{1,0:T(8,128)(2,1)S(1)} %bitcast.25, bf16[384,1152]{1,0:T(8,128)(2,1)S(1)} %copy-done.13, bf16[384,384]{1,0:T(8,128)(2,1)S(1)} %copy-done.14, bf16[384,1536]{1,0:T(8,128)(2,1)S(1)} %copy-done.9, bf16[1536,384]{1,0:T(8,128)(2,1)S(1)} %copy-done.11), custom_call_target="tpu_custom_call" | custom-call | flops 8999999488 | bytes 4000000 | tf_op jit(solution)/shard_map/pallas_call | solution.py:372
  94.4 4.6 %all-to-all-done.3 = bf16[32,32,384]{2,1,0:T(8,128)(2,1)S(1)} async-done(((bf16[32,32,384]{2,1,0:T(8,128)(2,1)}), bf16[32,32,384]{2,1,0:T(8,128)(2,1)S(1)}, u32[]{:S(2)}, u32[]{:S(2)}) %all-to-all-start.3) | async-done | bytes 786464 | tf_op jit(solution)/shard_map/all_to_all | solution.py:480
  99.0 3.2 %all-to-all-start.1 = ((bf16[32,32,384]{2,1,0:T(8,128)(2,1)}), bf16[32,32,384]{2,1,0:T(8,128)(2,1)S(1)}, u32[]{:S(2)}, u32[]{:S(2)}) async-start(bf16[32,32,384]{2,1,0:T(8,128)(2,1)} %bitcast.8), calls=%async_computation.1 | async-start | bytes 1572864 | tf_op jit(solution)/shard_map/all_to_all | solution.py:480
  102.1 0.0 copy-done
  102.1 1.2 shard_map.124.refs_2_
  103.3 19.6 %all-to-all-done.1 = bf16[32,32,384]{2,1,0:T(8,128)(2,1)S(1)} async-done(((bf16[32,32,384]{2,1,0:T(8,128)(2,1)}), bf16[32,32,384]{2,1,0:T(8,128)(2,1)S(1)}, u32[]{:S(2)}, u32[]{:S(2)}) %all-to-all-start.1) | async-done | bytes 786464 | tf_op jit(solution)/shard_map/all_to_all | solution.py:480
  123.0 1.2 shard_map.125
  (7 shorter events, 0.1 us)
Async XLA Ops:
  1.1 6.5 %collective-permute-start = (bf16[2,16,384]{2,1,0:T(8,128)(2,1)S(1)}, bf16[2,16,384]{2,1,0:T(8,128)(2,1)S(1)}, u32[]{:S(2)}, u32[]{:S(2)}) collective-permute-start(bf16[2,16,384]{2,1,0:T(8,128)(2,1)S(1)} %get-tuple-element.19), channel_id=1, source_target_pairs={{1,2},{2,1},{5,6},{6,5},{9,10},{10,9},{13,14},{14,13},{17,18},{18,... | collective-permute-start | bytes 73736 | tf_op jit(solution)/shard_map/ppermute | solution.py:433
  1.8 6.0 %collective-permute-start.1 = (bf16[2,16,384]{2,1,0:T(8,128)(2,1)S(1)}, bf16[2,16,384]{2,1,0:T(8,128)(2,1)S(1)}, u32[]{:S(2)}, u32[]{:S(2)}) collective-permute-start(bf16[2,16,384]{2,1,0:T(8,128)(2,1)S(1)} %get-tuple-element.20), channel_id=1, source_target_pairs={{0,1},{1,0},{2,3},{3,2},{4,5},{5,4},{6,7},{7,6},{8,9},{9,8},{10,11... | collective-permute-start | bytes 73736 | tf_op jit(solution)/shard_map/ppermute | solution.py:434
  7.9 9.8 %collective-permute-start.3 = (bf16[2,80,384]{2,1,0:T(8,128)(2,1)S(1)}, bf16[2,80,384]{2,1,0:T(8,128)(2,1)S(1)}, u32[]{:S(2)}, u32[]{:S(2)}) collective-permute-start(bf16[2,80,384]{2,1,0:T(8,128)(2,1)S(1)} %get-tuple-element.17), channel_id=1, source_target_pairs={{0,4},{4,0},{8,12},{12,8},{16,20},{20,16},{24,28},{28,24},{1,5},{5... | collective-permute-start | bytes 368648 | tf_op jit(solution)/shard_map/ppermute | solution.py:434
  9.8 7.9 %collective-permute-start.2 = (bf16[2,80,384]{2,1,0:T(8,128)(2,1)S(1)}, bf16[2,80,384]{2,1,0:T(8,128)(2,1)S(1)}, u32[]{:S(2)}, u32[]{:S(2)}) collective-permute-start(bf16[2,80,384]{2,1,0:T(8,128)(2,1)S(1)} %get-tuple-element.18), channel_id=1, source_target_pairs={{4,8},{12,16},{20,24},{8,4},{16,12},{24,20},{5,9},{13,17},{21,25},... | collective-permute-start | bytes 368648 | tf_op jit(solution)/shard_map/ppermute | solution.py:433
  12.8 1.4 %copy-start.1 = (bf16[2,16,64,384]{3,2,1,0:T(8,128)(2,1)S(1)}, bf16[2,16,64,384]{3,2,1,0:T(8,128)(2,1)}, u32[]{:S(2)}) copy-start(bf16[2,16,64,384]{3,2,1,0:T(8,128)(2,1)} %refs_0_.9) | copy-start | bytes 4718596
  14.2 1.3 %copy-start.3 = (bf16[384,1536]{1,0:T(8,128)(2,1)S(1)}, bf16[384,1536]{1,0:T(8,128)(2,1)}, u32[]{:S(2)}) copy-start(bf16[384,1536]{1,0:T(8,128)(2,1)} %refs_4_.6) | copy-start | bytes 3538948
  15.5 2.2 %copy-start.4 = (bf16[384,1536]{1,0:T(8,128)(2,1)S(1)}, bf16[384,1536]{1,0:T(8,128)(2,1)}, u32[]{:S(2)}) copy-start(bf16[384,1536]{1,0:T(8,128)(2,1)} %refs_4_.6) | copy-start | bytes 3538948
  15.5 2.2 %copy-start.7 = (bf16[1536,384]{1,0:T(8,128)(2,1)S(1)}, bf16[1536,384]{1,0:T(8,128)(2,1)}, u32[]{:S(2)}) copy-start(bf16[1536,384]{1,0:T(8,128)(2,1)} %refs_12_.3) | copy-start | bytes 3538948
  15.5 2.2 %copy-start.15 = (f32[3,3,1536]{2,1,0:T(4,128)S(1)}, f32[3,3,1536]{2,1,0:T(4,128)}, u32[]{:S(2)}) copy-start(f32[3,3,1536]{2,1,0:T(4,128)} %refs_5_.6) | copy-start | bytes 165892
  15.5 2.2 %copy-start.16 = (f32[1536]{0:T(1024)S(1)}, f32[1536]{0:T(1024)}, u32[]{:S(2)}) copy-start(f32[1536]{0:T(1024)} %refs_6_.3) | copy-start | bytes 18436
  15.5 2.2 %copy-start.17 = (s32[2,3]{1,0:T(2,128)S(1)}, s32[2,3]{1,0:T(2,128)}, u32[]{:S(2)}) copy-start(s32[2,3]{1,0:T(2,128)} %refs_0_.11) | copy-start | bytes 76
  15.5 2.2 %copy-start.18 = (bf16[128,128]{1,0:T(8,128)(2,1)S(1)}, bf16[128,128]{1,0:T(8,128)(2,1)}, u32[]{:S(2)}) copy-start(bf16[128,128]{1,0:T(8,128)(2,1)} %constant.33.clone.refs_7_) | copy-start | bytes 98308
  26.6 3.6 %copy-start.2 = (bf16[2,16,64,384]{3,2,1,0:T(8,128)(2,1)S(1)}, bf16[2,16,64,384]{3,2,1,0:T(8,128)(2,1)}, u32[]{:S(2)}) copy-start(bf16[2,16,64,384]{3,2,1,0:T(8,128)(2,1)} %refs_0_.9) | copy-start | bytes 4718596
  26.6 24.4 %all-to-all-start.2 = ((bf16[32,32,384]{2,1,0:T(8,128)(2,1)}), bf16[32,32,384]{2,1,0:T(8,128)(2,1)S(1)}, u32[]{:S(2)}, u32[]{:S(2)}) async-start(bf16[32,32,384]{2,1,0:T(8,128)(2,1)} %bitcast.10), calls=%async_computation.2 | async-start | bytes 1572864 | tf_op jit(solution)/shard_map/all_to_all | solution.py:480
  30.2 1.3 %copy-start.5 = (bf16[384,1536]{1,0:T(8,128)(2,1)S(1)}, bf16[384,1536]{1,0:T(8,128)(2,1)}, u32[]{:S(2)}) copy-start(bf16[384,1536]{1,0:T(8,128)(2,1)} %refs_4_.6) | copy-start | bytes 3538948
  31.5 2.1 %copy-start.6 = (bf16[384,1536]{1,0:T(8,128)(2,1)S(1)}, bf16[384,1536]{1,0:T(8,128)(2,1)}, u32[]{:S(2)}) copy-start(bf16[384,1536]{1,0:T(8,128)(2,1)} %refs_4_.6) | copy-start | bytes 3538948
  31.5 2.1 %copy-start.8 = (bf16[1536,384]{1,0:T(8,128)(2,1)S(1)}, bf16[1536,384]{1,0:T(8,128)(2,1)}, u32[]{:S(2)}) copy-start(bf16[1536,384]{1,0:T(8,128)(2,1)} %refs_12_.3) | copy-start | bytes 3538948
  42.4 11.8 %copy-start.9 = (bf16[384,1536]{1,0:T(8,128)(2,1)S(1)}, bf16[384,1536]{1,0:T(8,128)(2,1)}, u32[]{:S(2)}) copy-start(bf16[384,1536]{1,0:T(8,128)(2,1)} %refs_4_.7) | copy-start | bytes 3538948
  42.4 11.8 %copy-start.14 = (bf16[384,384]{1,0:T(8,128)(2,1)S(1)}, bf16[384,384]{1,0:T(8,128)(2,1)}, u32[]{:S(2)}) copy-start(bf16[384,384]{1,0:T(8,128)(2,1)} %refs_3_.3) | copy-start | bytes 884740
  51.0 24.0 %all-to-all-start = ((bf16[32,32,384]{2,1,0:T(8,128)(2,1)}), bf16[32,32,384]{2,1,0:T(8,128)(2,1)S(1)}, u32[]{:S(2)}, u32[]{:S(2)}) async-start(bf16[32,32,384]{2,1,0:T(8,128)(2,1)} %bitcast.6), calls=%async_computation | async-start | bytes 1572864 | tf_op jit(solution)/shard_map/all_to_all | solution.py:480
  54.2 1.3 %copy-start.10 = (bf16[1536,384]{1,0:T(8,128)(2,1)S(1)}, bf16[1536,384]{1,0:T(8,128)(2,1)}, u32[]{:S(2)}) copy-start(bf16[1536,384]{1,0:T(8,128)(2,1)} %refs_5_.7) | copy-start | bytes 3538948
  55.4 1.2 copy-start.12
  75.0 24.0 %all-to-all-start.3 = ((bf16[32,32,384]{2,1,0:T(8,128)(2,1)}), bf16[32,32,384]{2,1,0:T(8,128)(2,1)S(1)}, u32[]{:S(2)}, u32[]{:S(2)}) async-start(bf16[32,32,384]{2,1,0:T(8,128)(2,1)} %bitcast.12), calls=%async_computation.3 | async-start | bytes 1572864 | tf_op jit(solution)/shard_map/all_to_all | solution.py:480
  78.1 1.3 %copy-start.11 = (bf16[1536,384]{1,0:T(8,128)(2,1)S(1)}, bf16[1536,384]{1,0:T(8,128)(2,1)}, u32[]{:S(2)}) copy-start(bf16[1536,384]{1,0:T(8,128)(2,1)} %refs_5_.7) | copy-start | bytes 3538948
  79.4 1.2 copy-start.13
  94.4 7.8 %copy-start = (bf16[128,128]{1,0:T(8,128)(2,1)S(1)}, bf16[128,128]{1,0:T(8,128)(2,1)}, u32[]{:S(2)}) copy-start(bf16[128,128]{1,0:T(8,128)(2,1)} %constant.34.clone.refs_1_) | copy-start | bytes 98308
  99.0 24.0 %all-to-all-start.1 = ((bf16[32,32,384]{2,1,0:T(8,128)(2,1)}), bf16[32,32,384]{2,1,0:T(8,128)(2,1)S(1)}, u32[]{:S(2)}, u32[]{:S(2)}) async-start(bf16[32,32,384]{2,1,0:T(8,128)(2,1)} %bitcast.8), calls=%async_computation.1 | async-start | bytes 1572864 | tf_op jit(solution)/shard_map/all_to_all | solution.py:480

commit v4 on v2

--- a/solution.py
+++ b/solution.py
@@ -246,7 +246,7 @@
         branch = dot(jnp.concatenate(values, axis=0), project_ref[lanes])
         total[span] = branch if c == 0 else total[span] + branch
 
-    part = rows // 2
+    part = rows
     for c in range(hidden // CHUNK):
         expand_halo(c)
         if c == 0:

time: 125 us -> 125 us (level)
  no operation moved by 1% of the time
where the time goes in v4:
time: 125 us; the launch traced here: 124 us
  Pallas kernels  51.8 us (41%)
  waiting for transfers between devices  37.5 us (30%)
  starting transfers between devices  23.3 us (19%)
  local copies, waits for them, and re-layouts  11 us (9%)
    all_to_all x4, waiting for transfers between devices, exchange(): lax.all_to_all(message, ('ha', 'wa'), split_axis=0, concat_axis=0, tiled=...  37.3 us
    pallas_call x2, Pallas kernels, window_call(): pl.pallas_call(body, in_specs=[pl.BlockSpec(memory_space=pltpu.SMEM)] + [...  27.6 us
    pallas_call x2, Pallas kernels, conv_call(): pl.pallas_call(body, in_specs=[pl.BlockSpec(memory_space=pltpu.SMEM)] * 2...  17.6 us
    all_to_all x4, starting transfers between devices, exchange(): lax.all_to_all(message, ('ha', 'wa'), split_axis=0, concat_axis=0, tiled=...  13 us
    unnamed x38, local copies, waits for them, and re-layouts  8.86 us
    ppermute x2, starting transfers between devices, neighbours(): within = lax.ppermute(jnp.where(even, last, first), axis, inner)  6.62 us
    pallas_call x2, Pallas kernels, expand_call(): pl.pallas_call(body, in_specs=[pl.BlockSpec(memory_space=pltpu.VMEM)] * 2...  4.15 us
    ppermute x2, starting transfers between devices, neighbours(): across = lax.ppermute(jnp.where(even, first, last), axis, outer)  3.68 us
  transfers between devices with their start and end apart: 8, of which 5 were waited for; matrix products, arithmetic and copies ran while one was open for 1% of the time, Pallas kernels for 34%

profile of v4, /device:TPU:1, one launch (start us, length us, event | category | flops | bytes accessed | tf_op | source)
XLA Modules:
  0.0 124.2 jit_solution(5199205284556837956)
XLA Ops:
  0.0 1.1 fusion
  1.1 0.7 collective-permute-start
  1.8 4.7 %collective-permute-start.1 = (bf16[2,16,384]{2,1,0:T(8,128)(2,1)S(1)}, bf16[2,16,384]{2,1,0:T(8,128)(2,1)S(1)}, u32[]{:S(2)}, u32[]{:S(2)}) collective-permute-start(bf16[2,16,384]{2,1,0:T(8,128)(2,1)S(1)} %get-tuple-element.20), channel_id=1, source_target_pairs={{0,1},{1,0},{2,3},{3,2},{4,5},{5,4},{6,7},{7,6},{8,9},{9,8},{10,11... | collective-permute-start | bytes 73736 | tf_op jit(solution)/shard_map/ppermute | solution.py:428
  6.5 1.0 slice_bitcast_fusion.1
  7.5 0.1 pad.7.clone
  7.6 0.0 collective-permute-done.refs_10_
  7.6 0.1 collective-permute-done.1.refs_11_
  7.8 0.1 broadcast_select_fusion
  7.9 1.9 %collective-permute-start.3 = (bf16[2,80,384]{2,1,0:T(8,128)(2,1)S(1)}, bf16[2,80,384]{2,1,0:T(8,128)(2,1)S(1)}, u32[]{:S(2)}, u32[]{:S(2)}) collective-permute-start(bf16[2,80,384]{2,1,0:T(8,128)(2,1)S(1)} %get-tuple-element.17), channel_id=1, source_target_pairs={{0,4},{4,0},{8,12},{12,8},{16,20},{20,16},{24,28},{28,24},{1,5},{5... | collective-permute-start | bytes 368648 | tf_op jit(solution)/shard_map/ppermute | solution.py:428
  9.8 3.0 %collective-permute-start.2 = (bf16[2,80,384]{2,1,0:T(8,128)(2,1)S(1)}, bf16[2,80,384]{2,1,0:T(8,128)(2,1)S(1)}, u32[]{:S(2)}, u32[]{:S(2)}) collective-permute-start(bf16[2,80,384]{2,1,0:T(8,128)(2,1)S(1)} %get-tuple-element.18), channel_id=1, source_target_pairs={{4,8},{12,16},{20,24},{8,4},{16,12},{24,20},{5,9},{13,17},{21,25},... | collective-permute-start | bytes 368648 | tf_op jit(solution)/shard_map/ppermute | solution.py:427
  12.8 0.0 copy-start.1
  12.8 1.4 %copy-done.1 = bf16[2,16,64,384]{3,2,1,0:T(8,128)(2,1)S(1)} copy-done((bf16[2,16,64,384]{3,2,1,0:T(8,128)(2,1)S(1)}, bf16[2,16,64,384]{3,2,1,0:T(8,128)(2,1)}, u32[]{:S(2)}) %copy-start.1) | copy-done | bytes 1572888
  14.2 0.0 copy-start.3
  14.2 1.3 %copy-done.3 = bf16[384,1536]{1,0:T(8,128)(2,1)S(1)} copy-done((bf16[384,1536]{1,0:T(8,128)(2,1)S(1)}, bf16[384,1536]{1,0:T(8,128)(2,1)}, u32[]{:S(2)}) %copy-start.3) | copy-done | bytes 1179672
  15.5 0.0 copy-start.4
  15.5 0.0 copy-start.7
  15.5 0.0 copy-start.15
  15.5 0.0 copy-start.16
  15.5 0.0 copy-start.17
  15.5 0.0 copy-start.18
  15.6 2.1 %shard_map.121 = (f32[16,8,8,1536]{3,2,1,0:T(8,128)S(1)}, bf16[1024,384]{1,0:T(8,128)(2,1)S(1)}) custom-call(bf16[2,16,64,384]{3,2,1,0:T(8,128)(2,1)S(1)} %copy-done.1, bf16[384,1536]{1,0:T(8,128)(2,1)S(1)} %copy-done.3), custom_call_target="tpu_custom_call" | custom-call | flops 3000000000 | bytes 4000000 | tf_op jit(solution)/shard_map/pallas_call | solution.py:103
  17.6 0.1 add_convert_fusion.refs_1_
  17.7 0.0 collective-permute-done.3.refs_9_
  17.7 0.0 collective-permute-done.2.refs_8_
  17.7 0.0 copy-done.4
  17.7 0.0 copy-done.7
  17.7 0.0 copy-done.15
  17.7 0.0 copy-done.16
  17.8 0.0 copy-done.17
  17.8 0.0 copy-done.18
  17.8 8.8 %shard_map.122 = bf16[1024,384]{1,0:T(8,128)(2,1)} custom-call(s32[2,3]{1,0:T(2,128)S(1)} %copy-done.17, s32[2]{0:T(128)S(1)} %add_convert_fusion.refs_1_, f32[16,8,8,1536]{3,2,1,0:T(8,128)S(1)} %get-tuple-element.11.refs_2_, bf16[1024,384]{1,0:T(8,128)(2,1)S(1)} %get-tuple-element.12.refs_3_, bf16[384,1536]{1,0:T(8,128)(2,1)S(1)} %copy-done.4, ...), custom_call_target="tpu_custom_call" | custom-call | flops 4000000000 | bytes 4000000 | tf_op jit(solution)/shard_map/pallas_call | solution.py:295
  26.6 0.0 copy-start.2
  26.6 3.6 %all-to-all-start.2 = ((bf16[32,32,384]{2,1,0:T(8,128)(2,1)}), bf16[32,32,384]{2,1,0:T(8,128)(2,1)S(1)}, u32[]{:S(2)}, u32[]{:S(2)}) async-start(bf16[32,32,384]{2,1,0:T(8,128)(2,1)} %bitcast.10), calls=%async_computation.2 | async-start | bytes 1572864 | tf_op jit(solution)/shard_map/all_to_all | solution.py:474
  30.2 0.0 copy-done.2
  30.2 0.0 copy-start.5
  30.2 1.3 %copy-done.5 = bf16[384,1536]{1,0:T(8,128)(2,1)S(1)} copy-done((bf16[384,1536]{1,0:T(8,128)(2,1)S(1)}, bf16[384,1536]{1,0:T(8,128)(2,1)}, u32[]{:S(2)}) %copy-start.5) | copy-done | bytes 1179672
  31.5 0.0 copy-start.6
  31.5 2.1 %shard_map.118 = (f32[16,8,8,1536]{3,2,1,0:T(8,128)S(1)}, bf16[1024,384]{1,0:T(8,128)(2,1)S(1)}) custom-call(bf16[2,16,64,384]{3,2,1,0:T(8,128)(2,1)S(1)} %copy-done.2, bf16[384,1536]{1,0:T(8,128)(2,1)S(1)} %copy-done.5), custom_call_target="tpu_custom_call" | custom-call | flops 3000000000 | bytes 4000000 | tf_op jit(solution)/shard_map/pallas_call | solution.py:103
  33.5 0.0 copy-done.6
  33.6 0.0 copy-done.8
  33.6 8.8 %shard_map.119 = bf16[1024,384]{1,0:T(8,128)(2,1)} custom-call(s32[2,3]{1,0:T(2,128)S(1)} %copy-done.17, s32[2]{0:T(128)S(1)} %add_convert_fusion.refs_1_, f32[16,8,8,1536]{3,2,1,0:T(8,128)S(1)} %get-tuple-element.9.refs_2_, bf16[1024,384]{1,0:T(8,128)(2,1)S(1)} %get-tuple-element.10.refs_3_, bf16[384,1536]{1,0:T(8,128)(2,1)S(1)} %copy-done.6, ...), custom_call_target="tpu_custom_call" | custom-call | flops 4000000000 | bytes 4000000 | tf_op jit(solution)/shard_map/pallas_call | solution.py:295
  42.4 0.0 copy-start.9
  42.4 0.0 copy-start.14
  42.4 8.6 %all-to-all-done.2 = bf16[32,32,384]{2,1,0:T(8,128)(2,1)S(1)} async-done(((bf16[32,32,384]{2,1,0:T(8,128)(2,1)}), bf16[32,32,384]{2,1,0:T(8,128)(2,1)S(1)}, u32[]{:S(2)}, u32[]{:S(2)}) %all-to-all-start.2) | async-done | bytes 786464 | tf_op jit(solution)/shard_map/all_to_all | solution.py:474
  51.0 3.2 %all-to-all-start = ((bf16[32,32,384]{2,1,0:T(8,128)(2,1)}), bf16[32,32,384]{2,1,0:T(8,128)(2,1)S(1)}, u32[]{:S(2)}, u32[]{:S(2)}) async-start(bf16[32,32,384]{2,1,0:T(8,128)(2,1)} %bitcast.6), calls=%async_computation | async-start | bytes 1572864 | tf_op jit(solution)/shard_map/all_to_all | solution.py:474
  54.2 0.0 copy-done.9
  54.2 0.0 copy-done.14
  54.2 0.0 copy-start.10
  54.2 1.3 %copy-done.10 = bf16[1536,384]{1,0:T(8,128)(2,1)S(1)} copy-done((bf16[1536,384]{1,0:T(8,128)(2,1)S(1)}, bf16[1536,384]{1,0:T(8,128)(2,1)}, u32[]{:S(2)}) %copy-start.10) | copy-done | bytes 1179672
  55.4 0.0 copy-start.12
  55.5 1.2 copy-done.12
  56.6 13.8 %shard_map.123 = bf16[1024,384]{1,0:T(8,128)(2,1)} custom-call(s32[2,3]{1,0:T(2,128)S(1)} %copy-done.17, bf16[1024,384]{1,0:T(8,128)(2,1)S(1)} %bitcast.24, bf16[384,1152]{1,0:T(8,128)(2,1)S(1)} %copy-done.12, bf16[384,384]{1,0:T(8,128)(2,1)S(1)} %copy-done.14, bf16[384,1536]{1,0:T(8,128)(2,1)S(1)} %copy-done.9, bf16[1536,384]{1,0:T(8,128)(2,1)S(1)} %copy-done.10), custom_call_target="tpu_custom_call" | custom-call | flops 8999999488 | bytes 4000000 | tf_op jit(solution)/shard_map/pallas_call | solution.py:372
  70.4 4.6 %all-to-all-done = bf16[32,32,384]{2,1,0:T(8,128)(2,1)S(1)} async-done(((bf16[32,32,384]{2,1,0:T(8,128)(2,1)}), bf16[32,32,384]{2,1,0:T(8,128)(2,1)S(1)}, u32[]{:S(2)}, u32[]{:S(2)}) %all-to-all-start) | async-done | bytes 786464 | tf_op jit(solution)/shard_map/all_to_all | solution.py:474
  75.0 3.2 %all-to-all-start.3 = ((bf16[32,32,384]{2,1,0:T(8,128)(2,1)}), bf16[32,32,384]{2,1,0:T(8,128)(2,1)S(1)}, u32[]{:S(2)}, u32[]{:S(2)}) async-start(bf16[32,32,384]{2,1,0:T(8,128)(2,1)} %bitcast.12), calls=%async_computation.3 | async-start | bytes 1572864 | tf_op jit(solution)/shard_map/all_to_all | solution.py:474
  78.1 0.0 copy-start.11
  78.2 1.3 %copy-done.11 = bf16[1536,384]{1,0:T(8,128)(2,1)S(1)} copy-done((bf16[1536,384]{1,0:T(8,128)(2,1)S(1)}, bf16[1536,384]{1,0:T(8,128)(2,1)}, u32[]{:S(2)}) %copy-start.11) | copy-done | bytes 1179672
  79.4 1.2 copy-done.13
  80.6 13.8 %shard_map.120 = bf16[1024,384]{1,0:T(8,128)(2,1)} custom-call(s32[2,3]{1,0:T(2,128)S(1)} %copy-done.17, bf16[1024,384]{1,0:T(8,128)(2,1)S(1)} %bitcast.25, bf16[384,1152]{1,0:T(8,128)(2,1)S(1)} %copy-done.13, bf16[384,384]{1,0:T(8,128)(2,1)S(1)} %copy-done.14, bf16[384,1536]{1,0:T(8,128)(2,1)S(1)} %copy-done.9, bf16[1536,384]{1,0:T(8,128)(2,1)S(1)} %copy-done.11), custom_call_target="tpu_custom_call" | custom-call | flops 8999999488 | bytes 4000000 | tf_op jit(solution)/shard_map/pallas_call | solution.py:372
  94.4 4.6 %all-to-all-done.3 = bf16[32,32,384]{2,1,0:T(8,128)(2,1)S(1)} async-done(((bf16[32,32,384]{2,1,0:T(8,128)(2,1)}), bf16[32,32,384]{2,1,0:T(8,128)(2,1)S(1)}, u32[]{:S(2)}, u32[]{:S(2)}) %all-to-all-start.3) | async-done | bytes 786464 | tf_op jit(solution)/shard_map/all_to_all | solution.py:474
  99.0 3.2 %all-to-all-start.1 = ((bf16[32,32,384]{2,1,0:T(8,128)(2,1)}), bf16[32,32,384]{2,1,0:T(8,128)(2,1)S(1)}, u32[]{:S(2)}, u32[]{:S(2)}) async-start(bf16[32,32,384]{2,1,0:T(8,128)(2,1)} %bitcast.8), calls=%async_computation.1 | async-start | bytes 1572864 | tf_op jit(solution)/shard_map/all_to_all | solution.py:474
  102.1 0.0 copy-done
  102.1 1.2 %shard_map.124.rest_0_ = bf16[2,16,64,384]{3,2,1,0:T(8,128)(2,1)} custom-call(bf16[1024,384]{1,0:T(8,128)(2,1)S(1)} %bitcast.22, bf16[128,128]{1,0:T(8,128)(2,1)S(1)} %copy-done), custom_call_target="tpu_custom_call" | custom-call | flops 100000000 | bytes 2000000 | tf_op jit(solution)/shard_map/pallas_call | solution.py:409
  103.4 19.6 %all-to-all-done.1 = bf16[32,32,384]{2,1,0:T(8,128)(2,1)S(1)} async-done(((bf16[32,32,384]{2,1,0:T(8,128)(2,1)}), bf16[32,32,384]{2,1,0:T(8,128)(2,1)S(1)}, u32[]{:S(2)}, u32[]{:S(2)}) %all-to-all-start.1) | async-done | bytes 786464 | tf_op jit(solution)/shard_map/all_to_all | solution.py:474
  123.0 1.2 %shard_map.125 = bf16[2,16,64,384]{3,2,1,0:T(8,128)(2,1)} custom-call(bf16[1024,384]{1,0:T(8,128)(2,1)S(1)} %bitcast.23, bf16[128,128]{1,0:T(8,128)(2,1)S(1)} %copy-done, bf16[2,16,64,384]{3,2,1,0:T(8,128)(2,1)} %shard_map.124.rest_0_), custom_call_target="tpu_custom_call", output_to_operand_aliasing={{}: (2, {})} | custom-call | flops 100000000 | bytes 2000000 | tf_op jit(solution)/shard_map/pallas_call | solution.py:409
  (7 shorter events, 0.1 us)
Async XLA Ops:
  1.1 6.5 %collective-permute-start = (bf16[2,16,384]{2,1,0:T(8,128)(2,1)S(1)}, bf16[2,16,384]{2,1,0:T(8,128)(2,1)S(1)}, u32[]{:S(2)}, u32[]{:S(2)}) collective-permute-start(bf16[2,16,384]{2,1,0:T(8,128)(2,1)S(1)} %get-tuple-element.19), channel_id=1, source_target_pairs={{1,2},{2,1},{5,6},{6,5},{9,10},{10,9},{13,14},{14,13},{17,18},{18,... | collective-permute-start | bytes 73736 | tf_op jit(solution)/shard_map/ppermute | solution.py:427
  1.8 6.0 %collective-permute-start.1 = (bf16[2,16,384]{2,1,0:T(8,128)(2,1)S(1)}, bf16[2,16,384]{2,1,0:T(8,128)(2,1)S(1)}, u32[]{:S(2)}, u32[]{:S(2)}) collective-permute-start(bf16[2,16,384]{2,1,0:T(8,128)(2,1)S(1)} %get-tuple-element.20), channel_id=1, source_target_pairs={{0,1},{1,0},{2,3},{3,2},{4,5},{5,4},{6,7},{7,6},{8,9},{9,8},{10,11... | collective-permute-start | bytes 73736 | tf_op jit(solution)/shard_map/ppermute | solution.py:428
  7.9 9.8 %collective-permute-start.3 = (bf16[2,80,384]{2,1,0:T(8,128)(2,1)S(1)}, bf16[2,80,384]{2,1,0:T(8,128)(2,1)S(1)}, u32[]{:S(2)}, u32[]{:S(2)}) collective-permute-start(bf16[2,80,384]{2,1,0:T(8,128)(2,1)S(1)} %get-tuple-element.17), channel_id=1, source_target_pairs={{0,4},{4,0},{8,12},{12,8},{16,20},{20,16},{24,28},{28,24},{1,5},{5... | collective-permute-start | bytes 368648 | tf_op jit(solution)/shard_map/ppermute | solution.py:428
  9.8 7.9 %collective-permute-start.2 = (bf16[2,80,384]{2,1,0:T(8,128)(2,1)S(1)}, bf16[2,80,384]{2,1,0:T(8,128)(2,1)S(1)}, u32[]{:S(2)}, u32[]{:S(2)}) collective-permute-start(bf16[2,80,384]{2,1,0:T(8,128)(2,1)S(1)} %get-tuple-element.18), channel_id=1, source_target_pairs={{4,8},{12,16},{20,24},{8,4},{16,12},{24,20},{5,9},{13,17},{21,25},... | collective-permute-start | bytes 368648 | tf_op jit(solution)/shard_map/ppermute | solution.py:427
  12.8 1.4 %copy-start.1 = (bf16[2,16,64,384]{3,2,1,0:T(8,128)(2,1)S(1)}, bf16[2,16,64,384]{3,2,1,0:T(8,128)(2,1)}, u32[]{:S(2)}) copy-start(bf16[2,16,64,384]{3,2,1,0:T(8,128)(2,1)} %refs_0_.9) | copy-start | bytes 4718596
  14.2 1.3 %copy-start.3 = (bf16[384,1536]{1,0:T(8,128)(2,1)S(1)}, bf16[384,1536]{1,0:T(8,128)(2,1)}, u32[]{:S(2)}) copy-start(bf16[384,1536]{1,0:T(8,128)(2,1)} %refs_4_.6) | copy-start | bytes 3538948
  15.5 2.2 %copy-start.4 = (bf16[384,1536]{1,0:T(8,128)(2,1)S(1)}, bf16[384,1536]{1,0:T(8,128)(2,1)}, u32[]{:S(2)}) copy-start(bf16[384,1536]{1,0:T(8,128)(2,1)} %refs_4_.6) | copy-start | bytes 3538948
  15.5 2.2 %copy-start.7 = (bf16[1536,384]{1,0:T(8,128)(2,1)S(1)}, bf16[1536,384]{1,0:T(8,128)(2,1)}, u32[]{:S(2)}) copy-start(bf16[1536,384]{1,0:T(8,128)(2,1)} %refs_12_.3) | copy-start | bytes 3538948
  15.5 2.2 %copy-start.15 = (f32[3,3,1536]{2,1,0:T(4,128)S(1)}, f32[3,3,1536]{2,1,0:T(4,128)}, u32[]{:S(2)}) copy-start(f32[3,3,1536]{2,1,0:T(4,128)} %refs_5_.6) | copy-start | bytes 165892
  15.5 2.2 %copy-start.16 = (f32[1536]{0:T(1024)S(1)}, f32[1536]{0:T(1024)}, u32[]{:S(2)}) copy-start(f32[1536]{0:T(1024)} %refs_6_.3) | copy-start | bytes 18436
  15.5 2.2 %copy-start.17 = (s32[2,3]{1,0:T(2,128)S(1)}, s32[2,3]{1,0:T(2,128)}, u32[]{:S(2)}) copy-start(s32[2,3]{1,0:T(2,128)} %refs_0_.11) | copy-start | bytes 76
  15.5 2.2 %copy-start.18 = (bf16[128,128]{1,0:T(8,128)(2,1)S(1)}, bf16[128,128]{1,0:T(8,128)(2,1)}, u32[]{:S(2)}) copy-start(bf16[128,128]{1,0:T(8,128)(2,1)} %constant.33.clone.refs_7_) | copy-start | bytes 98308
  26.6 3.6 %copy-start.2 = (bf16[2,16,64,384]{3,2,1,0:T(8,128)(2,1)S(1)}, bf16[2,16,64,384]{3,2,1,0:T(8,128)(2,1)}, u32[]{:S(2)}) copy-start(bf16[2,16,64,384]{3,2,1,0:T(8,128)(2,1)} %refs_0_.9) | copy-start | bytes 4718596
  26.6 24.4 %all-to-all-start.2 = ((bf16[32,32,384]{2,1,0:T(8,128)(2,1)}), bf16[32,32,384]{2,1,0:T(8,128)(2,1)S(1)}, u32[]{:S(2)}, u32[]{:S(2)}) async-start(bf16[32,32,384]{2,1,0:T(8,128)(2,1)} %bitcast.10), calls=%async_computation.2 | async-start | bytes 1572864 | tf_op jit(solution)/shard_map/all_to_all | solution.py:474
  30.2 1.3 %copy-start.5 = (bf16[384,1536]{1,0:T(8,128)(2,1)S(1)}, bf16[384,1536]{1,0:T(8,128)(2,1)}, u32[]{:S(2)}) copy-start(bf16[384,1536]{1,0:T(8,128)(2,1)} %refs_4_.6) | copy-start | bytes 3538948
  31.5 2.1 %copy-start.6 = (bf16[384,1536]{1,0:T(8,128)(2,1)S(1)}, bf16[384,1536]{1,0:T(8,128)(2,1)}, u32[]{:S(2)}) copy-start(bf16[384,1536]{1,0:T(8,128)(2,1)} %refs_4_.6) | copy-start | bytes 3538948
  31.5 2.1 %copy-start.8 = (bf16[1536,384]{1,0:T(8,128)(2,1)S(1)}, bf16[1536,384]{1,0:T(8,128)(2,1)}, u32[]{:S(2)}) copy-start(bf16[1536,384]{1,0:T(8,128)(2,1)} %refs_12_.3) | copy-start | bytes 3538948
  42.4 11.8 %copy-start.9 = (bf16[384,1536]{1,0:T(8,128)(2,1)S(1)}, bf16[384,1536]{1,0:T(8,128)(2,1)}, u32[]{:S(2)}) copy-start(bf16[384,1536]{1,0:T(8,128)(2,1)} %refs_4_.7) | copy-start | bytes 3538948
  42.4 11.8 %copy-start.14 = (bf16[384,384]{1,0:T(8,128)(2,1)S(1)}, bf16[384,384]{1,0:T(8,128)(2,1)}, u32[]{:S(2)}) copy-start(bf16[384,384]{1,0:T(8,128)(2,1)} %refs_3_.3) | copy-start | bytes 884740
  51.0 24.0 %all-to-all-start = ((bf16[32,32,384]{2,1,0:T(8,128)(2,1)}), bf16[32,32,384]{2,1,0:T(8,128)(2,1)S(1)}, u32[]{:S(2)}, u32[]{:S(2)}) async-start(bf16[32,32,384]{2,1,0:T(8,128)(2,1)} %bitcast.6), calls=%async_computation | async-start | bytes 1572864 | tf_op jit(solution)/shard_map/all_to_all | solution.py:474
  54.2 1.3 %copy-start.10 = (bf16[1536,384]{1,0:T(8,128)(2,1)S(1)}, bf16[1536,384]{1,0:T(8,128)(2,1)}, u32[]{:S(2)}) copy-start(bf16[1536,384]{1,0:T(8,128)(2,1)} %refs_5_.7) | copy-start | bytes 3538948
  55.4 1.2 copy-start.12
  75.0 24.0 %all-to-all-start.3 = ((bf16[32,32,384]{2,1,0:T(8,128)(2,1)}), bf16[32,32,384]{2,1,0:T(8,128)(2,1)S(1)}, u32[]{:S(2)}, u32[]{:S(2)}) async-start(bf16[32,32,384]{2,1,0:T(8,128)(2,1)} %bitcast.12), calls=%async_computation.3 | async-start | bytes 1572864 | tf_op jit(solution)/shard_map/all_to_all | solution.py:474
  78.1 1.3 %copy-start.11 = (bf16[1536,384]{1,0:T(8,128)(2,1)S(1)}, bf16[1536,384]{1,0:T(8,128)(2,1)}, u32[]{:S(2)}) copy-start(bf16[1536,384]{1,0:T(8,128)(2,1)} %refs_5_.7) | copy-start | bytes 3538948
  79.4 1.2 copy-start.13
  94.4 7.8 %copy-start = (bf16[128,128]{1,0:T(8,128)(2,1)S(1)}, bf16[128,128]{1,0:T(8,128)(2,1)}, u32[]{:S(2)}) copy-start(bf16[128,128]{1,0:T(8,128)(2,1)} %constant.34.clone.order_ref) | copy-start | bytes 98308
  99.0 24.0 %all-to-all-start.1 = ((bf16[32,32,384]{2,1,0:T(8,128)(2,1)}), bf16[32,32,384]{2,1,0:T(8,128)(2,1)S(1)}, u32[]{:S(2)}, u32[]{:S(2)}) async-start(bf16[32,32,384]{2,1,0:T(8,128)(2,1)} %bitcast.8), calls=%async_computation.1 | async-start | bytes 1572864 | tf_op jit(solution)/shard_map/all_to_all | solution.py:474
